TPU v7x, 256 devices: a whole 4x4x8 slice. The times are simulated.
256 devices in a mesh: band: 128 (over x_hi, y, z, core), grid: 2 (over x_lo).
Axes of the slice: x: 4 (x_hi: 2, x_lo: 2; x = x_hi * 2 + x_lo), y: 4, z: 8, core: 2. Of those that a mesh axis runs over, the one named last changes fastest.
Arguments:
- orbitals: float32 [128, 72, 5184], P('band', 'grid'), may hold values from -6 to 6
- owners: int32 [128], replicated, may hold values from 0 to 127, each once
Outputs:
- exchange_field: float32 [2, 128, 186624], P('grid', None, 'band')
- intersection: float32 [128, 128], replicated
Inputs may be any that keep to these rules, and one draw needn't show every extreme that they name: owners holds every index of the band axis exactly once; only its first 2 entries are used.
All inputs are finite; a program needn't handle non-finite values.
Results may differ from a plain program's by a relative error of at most 0.00019.
Values sent between devices are 32-bit elements; how exact they have to be, the bound alone decides.
A program may use at most 64 MiB of HBM per device.

v0:
```python
import math

import jax
import jax.numpy as jnp
from jax import lax
from jax.sharding import PartitionSpec as P

NX = 72
NY = 72
NZ = 72
ROUNDS = 2


HIGHEST_PRECISION = lax.Precision.HIGHEST
EXCHANGE_FRACTION = 0.25


def from_root(block, axis, source):
    block = jnp.where(lax.axis_index(axis) == source, block, jnp.zeros_like(block))
    return lax.psum(block, axis)


def real_table(length):
    positions = jnp.arange(length, dtype=jnp.int32)
    nyquist = length // 2
    frequency = jnp.where(positions <= nyquist, positions, positions - nyquist)
    phase_int = frequency[:, None] * positions[None, :] % length
    angles = phase_int.astype(jnp.float32) * (2.0 * math.pi / length)
    weights = jnp.where(
        (positions == 0) | (positions == nyquist), 1.0 / math.sqrt(length), math.sqrt(2.0 / length)
    ).astype(jnp.float32)
    basis = (
        jnp.where((positions <= nyquist)[:, None], jnp.cos(angles), jnp.sin(angles))
        * weights[:, None]
    )
    wavenum = frequency.astype(jnp.float32) * (2.0 * math.pi / length)
    return (basis, wavenum * wavenum)


def shards(orbitals, owners):
    band_count, local_x, plane_size = orbitals.shape
    tab_x, sq_x = real_table(NX)
    tab_y, sq_y = real_table(NY)
    tab_z, sq_z = real_table(NZ)
    total_sq = sq_x[:, None, None] + sq_y[None, :, None] + sq_z[None, None, :]
    positive = total_sq > 0
    kernel = jnp.where(positive, math.pi / jnp.where(positive, total_sq, 1.0), 0.0)
    grid_slot = lax.axis_index("grid")
    pair_count = band_count * band_count
    potential_sum = jnp.zeros(orbitals.shape, jnp.float32)
    for round_index in range(ROUNDS):
        lent_block = from_root(orbitals, "band", owners[round_index])
        density = (orbitals[:, None] * lent_block[None]).reshape(pair_count, local_x, NY, NZ)
        spectrum = jnp.einsum("by,pxyz->pxbz", tab_y, density, precision=HIGHEST_PRECISION)
        spectrum = jnp.einsum("cz,pxbz->pxbc", tab_z, spectrum, precision=HIGHEST_PRECISION)
        columns = lax.all_to_all(spectrum, "grid", split_axis=2, concat_axis=1, tiled=True)
        width_y = columns.shape[2]
        kernel_part = lax.dynamic_slice_in_dim(kernel, grid_slot * width_y, width_y, 1)
        scaled = (
            jnp.einsum("ax,pxyz->payz", tab_x, columns, precision=HIGHEST_PRECISION)
            * kernel_part[None]
        )
        returned = jnp.einsum("ax,payz->pxyz", tab_x, scaled, precision=HIGHEST_PRECISION)
        spectrum = lax.all_to_all(returned, "grid", split_axis=1, concat_axis=2, tiled=True)
        potential = jnp.einsum("by,pxbz->pxyz", tab_y, spectrum, precision=HIGHEST_PRECISION)
        potential = jnp.einsum("cz,pxyc->pxyz", tab_z, potential, precision=HIGHEST_PRECISION)
        potential = potential.reshape(band_count, band_count, local_x, plane_size)
        potential_sum = potential_sum - EXCHANGE_FRACTION * jnp.sum(
            lent_block[None] * potential, axis=1
        )
    flat_field = potential_sum.reshape(band_count, local_x * plane_size)
    orb_cols, field_cols = (
        lax.all_to_all(
            orbitals.reshape(band_count, local_x * plane_size),
            "band",
            split_axis=1,
            concat_axis=0,
            tiled=True,
        ),
        lax.all_to_all(flat_field, "band", split_axis=1, concat_axis=0, tiled=True),
    )
    partial_intersection = jnp.dot(
        orb_cols, field_cols.T, precision=HIGHEST_PRECISION, preferred_element_type=jnp.float32
    ) / (NX * NY * NZ)
    intersection = lax.psum(partial_intersection, ("band", "grid"))
    return (field_cols[None], intersection)


def solution(mesh):
    in_specs = (P("band", "grid", None), P())
    out_specs = (P("grid", None, "band"), P())
    return jax.shard_map(shards, mesh=mesh, in_specs=in_specs, out_specs=out_specs, check_vma=False)
```

profile of v0, /device:TPU:1, one launch (start us, length us, event | category | flops | bytes accessed | tf_op | source)
XLA Modules:
  0.0 1651.1 jit_solution(17105419638907169033)
XLA Ops:
  7.2 0.0 all-reduce.6.cloned.1.call-start
  7.2 1.3 fusion.65
  9.8 2.4 copy_select_fusion.1
  12.3 0.0 all-reduce.6.cloned.1.call-update
  12.3 1.1 copy-done
  13.4 1.8 reduce
  15.2 2.2 all_to_all.87
  17.4 0.1 broadcast_add_fusion
  17.5 1232.3 %all-reduce.6.cloned.1.call-done = (f32[1,36,5184]{2,1,0:T(8,128)}, f32[1,36,5184]{2,1,0:T(8,128)}) async-done(((f32[1,36,5184]{2,1,0:T(8,128)}, f32[1,36,5184]{2,1,0:T(8,128)}), (f32[1,36,5184]{2,1,0:T(8,128)}, f32[1,36,5184]{2,1,0:T(8,128)})) %all-reduce.6.cloned.1.call-update) | async-done | bytes 1493008 | tf_op jit(solution)/shard_map/psum | solution.py:20
  1249.8 1.6 copy_multiply_fusion.1
  1251.3 0.6 mul.269
  1252.0 2.3 convolution_bitcast_fusion.9
  1254.3 2.3 convolution_bitcast_fusion.8
  1256.6 2.4 copy.123
  1259.1 4.1 all-to-all-start
  1263.2 0.6 mul.283
  1263.8 2.3 convolution_bitcast_fusion.4
  1266.1 2.3 convolution_bitcast_fusion.3
  1268.5 2.5 copy.135
  1270.9 5.6 all-to-all-done
  1276.5 3.8 all-to-all-start.2
  1280.3 0.9 copy.124
  1281.2 0.3 copy.125
  1281.5 1.2 reshape.222
  1282.6 3.9 fusion.1
  1286.5 1.4 convolution_bitcast_fusion.6
  1287.9 2.1 copy.127
  1290.1 2.6 all-to-all-done.2
  1292.7 3.6 all-to-all-start.1
  1296.3 0.9 copy.136
  1297.2 0.3 copy.137
  1297.5 1.2 reshape.226
  1298.7 3.9 fusion.3
  1302.6 1.4 convolution_bitcast_fusion.1
  1304.0 2.1 copy.139
  1306.1 1.6 all-to-all-done.1
  1307.8 4.7 all-to-all-start.3
  1312.5 0.1 copy.128
  1312.6 0.1 reshape.224
  1312.7 2.3 convolution_bitcast_fusion.5
  1315.1 2.3 fusion.19
  1317.4 5.8 all-to-all-done.3
  1323.2 26.1 %all-to-all-start.5 = ((f32[1,128,1458]{2,0,1:T(1,128)}), f32[1,128,1458]{2,0,1:T(1,128)}, u32[]{:S(2)}, u32[]{:S(2)}) async-start(f32[1,128,1458]{2,0,1:T(1,128)} %all_to_all.87), calls=%async_computation.5 | async-start | bytes 1572864 | tf_op jit(solution)/shard_map/all_to_all | solution.py:73
  1349.3 1.4 copy.140
  1350.7 1.2 reshape.228
  1351.9 3.6 convolution_bitcast_fusion
  1355.6 2.3 fusion.12
  1357.9 1.4 reshape.213
  1359.3 1.4 reshape.219
  1360.7 0.0 copy-done.1
  1360.7 0.1 copy-done.2
  1360.8 1.6 multiply_subtract_fusion
  1362.4 2.2 all_to_all.86
  1364.5 9.6 all-to-all-done.5
  1374.2 7.1 all-to-all-start.4
  1381.3 0.0 all-reduce.4.cloned.1.call-start
  1381.3 2.5 copy.146
  1383.8 22.8 %all-to-all-done.4 = f32[1,128,1458]{2,0,1:T(1,128)S(1)} async-done(((f32[1,128,1458]{2,0,1:T(1,128)}), f32[1,128,1458]{2,0,1:T(1,128)S(1)}, u32[]{:S(2)}, u32[]{:S(2)}) %all-to-all-start.4) | async-done | bytes 746528 | tf_op jit(solution)/shard_map/all_to_all | solution.py:80
  1406.6 0.9 copy.144
  1407.5 2.1 fusion.7
  1409.6 0.0 all-reduce.4.cloned.1.call-update
  1409.6 1.9 copy.147
  1411.6 230.7 %all-reduce.4.cloned.1.call-done = f32[128,128]{0,1:T(8,128)} async-done(((f32[128,128]{0,1:T(8,128)}), f32[128,128]{0,1:T(8,128)}) %all-reduce.4.cloned.1.call-update) | async-done | bytes 65552 | tf_op jit(solution)/shard_map/psum | solution.py:85
  1642.3 1.6 copy.148
  (7 shorter events, 0.0 us)
Async XLA Ops:
  7.2 1242.6 %all-reduce.6.cloned.1.call-start = ((), (), s32[]{:S(2)}) async-start(), calls=%async_computation.7 | async-start | bytes 3358720 | tf_op jit(solution)/shard_map/psum | solution.py:20
  12.3 1.1 copy-start
  1259.1 17.4 %all-to-all-start = ((f32[1,36,72,72]{3,0,1,2:T(1,128)}), f32[1,36,72,72]{3,0,1,2:T(1,128)S(1)}, u32[]{:S(2)}, u32[]{:S(2)}) async-start(f32[1,36,72,72]{3,0,1,2:T(1,128)} %copy.123), calls=%async_computation | async-start | bytes 2654208 | tf_op jit(solution)/shard_map/all_to_all | solution.py:56
  1276.5 16.2 all-to-all-start.2
  1292.7 15.1 all-to-all-start.1
  1307.8 15.4 all-to-all-start.3
  1323.2 51.0 %all-to-all-start.5 = ((f32[1,128,1458]{2,0,1:T(1,128)}), f32[1,128,1458]{2,0,1:T(1,128)}, u32[]{:S(2)}, u32[]{:S(2)}) async-start(f32[1,128,1458]{2,0,1:T(1,128)} %all_to_all.87), calls=%async_computation.5 | async-start | bytes 1572864 | tf_op jit(solution)/shard_map/all_to_all | solution.py:73
  1359.3 1.4 copy-start.1
  1359.3 1.5 copy-start.2
  1374.2 32.4 %all-to-all-start.4 = ((f32[1,128,1458]{2,0,1:T(1,128)}), f32[1,128,1458]{2,0,1:T(1,128)S(1)}, u32[]{:S(2)}, u32[]{:S(2)}) async-start(f32[1,128,1458]{2,0,1:T(1,128)} %all_to_all.86), calls=%async_computation.4 | async-start | bytes 1572864 | tf_op jit(solution)/shard_map/all_to_all | solution.py:80
  1381.3 261.0 %all-reduce.4.cloned.1.call-start = ((), (), s32[]{:S(2)}) async-start(), calls=%async_computation.6 | async-start | bytes 131072 | tf_op jit(solution)/shard_map/psum | solution.py:85
Sparse Core Ops, SparseCore 0:
  12.4 1237.3 all-reduce.5
  1409.8 232.4 all-reduce.3
where the time goes:
time: 1660 us; the launch traced here: 1650 us
  waiting for transfers between devices  1510 us (91%)
  starting transfers between devices  49.6 us (3%)
  local copies, waits for them, and re-layouts  34.5 us (2%)
  matrix products  32.6 us (2%)
    psum x1, waiting for transfers between devices, from_root(): return lax.psum(block, axis)  1230 us
    psum x1, waiting for transfers between devices, shards(): intersection = lax.psum(partial_intersection, ('band', 'grid'))  231 us
  transfers between devices with their start and end apart: 8, of which 8 were waited for; matrix products, arithmetic and copies ran while one was open for 3% of the time, Pallas kernels for 0%

commit v1 on v0

v1 whole, which is shorter than its diff:
```python
import math

import jax
import jax.numpy as jnp
from jax import lax
from jax.sharding import PartitionSpec as P

NX = 72
NY = 72
NZ = 72


HIGHEST_PRECISION = lax.Precision.HIGHEST
EXCHANGE_FRACTION = 0.25


def real_table(length):
    positions = jnp.arange(length, dtype=jnp.int32)
    nyquist = length // 2
    frequency = jnp.where(positions <= nyquist, positions, positions - nyquist)
    phase_int = frequency[:, None] * positions[None, :] % length
    angles = phase_int.astype(jnp.float32) * (2.0 * math.pi / length)
    weights = jnp.where(
        (positions == 0) | (positions == nyquist), 1.0 / math.sqrt(length), math.sqrt(2.0 / length)
    ).astype(jnp.float32)
    basis = (
        jnp.where((positions <= nyquist)[:, None], jnp.cos(angles), jnp.sin(angles))
        * weights[:, None]
    )
    wavenum = frequency.astype(jnp.float32) * (2.0 * math.pi / length)
    return (basis, wavenum * wavenum)


def shards(orbitals, owners):
    _, local_x, plane_size = orbitals.shape
    table, sq = real_table(NX)
    total_sq = sq[:, None, None] + sq[None, :, None] + sq[None, None, :]
    positive = total_sq > 0
    kernel = jnp.where(positive, math.pi / jnp.where(positive, total_sq, 1.0), 0.0)
    slot = lax.axis_index("grid")
    swap = [(0, 1), (1, 0)]

    orb_cols = lax.all_to_all(
        orbitals.reshape(1, local_x * plane_size), "band", split_axis=1, concat_axis=0, tiled=True
    )
    picked = jnp.concatenate(
        [lax.dynamic_slice_in_dim(orb_cols, owners[r], 1, 0) for r in range(2)], axis=0
    )
    picked = lax.all_to_all(picked, "grid", split_axis=0, concat_axis=0, tiled=True)
    lent = lax.all_gather(picked, "band", axis=0, tiled=False)
    lent = jnp.swapaxes(lent, 0, 1).reshape(NX, NY, NZ)

    other = lax.ppermute(orbitals[0], "grid", swap)
    mine = orbitals[0]
    own = jnp.where(
        slot == 0, jnp.concatenate([mine, other], 0), jnp.concatenate([other, mine], 0)
    ).reshape(NX, NY, NZ)

    values = own * lent
    values = jnp.einsum("by,xyz->xbz", table, values, precision=HIGHEST_PRECISION)
    values = jnp.einsum("cz,xbz->xbc", table, values, precision=HIGHEST_PRECISION)
    values = jnp.einsum("ax,xyz->ayz", table, values, precision=HIGHEST_PRECISION) * kernel
    values = jnp.einsum("ax,ayz->xyz", table, values, precision=HIGHEST_PRECISION)
    values = jnp.einsum("by,xbz->xyz", table, values, precision=HIGHEST_PRECISION)
    values = jnp.einsum("cz,xyc->xyz", table, values, precision=HIGHEST_PRECISION)
    part = (-EXCHANGE_FRACTION * lent * values).reshape(2, local_x * plane_size)
    keep = lax.dynamic_slice_in_dim(part, slot, 1, 0)
    give = lax.dynamic_slice_in_dim(part, 1 - slot, 1, 0)
    field = keep + lax.ppermute(give, "grid", swap)

    field_cols = lax.all_to_all(field, "band", split_axis=1, concat_axis=0, tiled=True)
    partial = jnp.dot(
        orb_cols, field_cols.T, precision=HIGHEST_PRECISION, preferred_element_type=jnp.float32
    ) / (NX * NY * NZ)
    pieces = lax.all_to_all(partial, "band", split_axis=0, concat_axis=0, tiled=True)
    row = jnp.sum(pieces, axis=0, keepdims=True)
    row = row + lax.ppermute(row, "grid", swap)
    intersection = lax.all_to_all(
        jnp.broadcast_to(row, (128, 128)), "band", split_axis=0, concat_axis=0, tiled=True
    )
    return (field_cols[None], intersection)


def solution(mesh):
    in_specs = (P("band", "grid", None), P())
    out_specs = (P("grid", None, "band"), P())
    return jax.shard_map(shards, mesh=mesh, in_specs=in_specs, out_specs=out_specs, check_vma=False)
```

time: 1660 us -> 333 us (0.20)
  waiting for transfers between devices: 1510 us -> 173 us
  blocking collectives: 0 us -> 24.8 us
    psum x2 -> x0, waiting for transfers between devices: 1460 us -> none  [the longest x1 1230 us: from_root(): return lax.psum(block, axis)]
    all_gather x0 -> x1, waiting for transfers between devices: none -> 80.5 us  [shards(): lent = lax.all_gather(picked, 'band', axis=0, tiled=False)]
    ppermute x0 -> x3, waiting for transfers between devices: none -> 36.6 us  [the longest x1 17.9 us: shards(): field = keep + lax.ppermute(give, 'grid', swap)]
    all_to_all x0 -> x2, blocking collectives: none -> 24.8 us  [the longest x1 19.1 us: shards(): lax.all_to_all(partial, 'band', split_axis=0, concat_axis=0, tiled=True)]
    all_to_all x6 -> x3, starting transfers between devices: 49.5 us -> 34 us  [the longest x1 16.4 us: shards(): lax.all_to_all(orbitals.reshape(1, local_x * plane_size), 'band', split_a...]
    all_to_all x6 -> x3, waiting for transfers between devices: 47.9 us -> 55.4 us  [the longest x1 24.4 us: shards(): lax.all_to_all(field, 'band', split_axis=1, concat_axis=0, tiled=True)]
  transfers between devices with their start and end apart: 8 -> 7, of which waited for: 8 -> 7; matrix products, arithmetic and copies ran while one was open for 3% -> 2% of each run, Pallas kernels for 0% -> 0%
where the time goes in v1:
time: 333 us; the launch traced here: 328 us
  waiting for transfers between devices  173 us (52%)
  starting transfers between devices  35.3 us (11%)
  matrix products  31.5 us (9%)
  local copies, waits for them, and re-layouts  27.9 us (8%)
  blocking collectives  24.8 us (7%)
  between operations  18.3 us (5%)
  other arithmetic  17.3 us (5%)
    all_gather x1, waiting for transfers between devices, shards(): lent = lax.all_gather(picked, 'band', axis=0, tiled=False)  80.5 us
    all_to_all x1, waiting for transfers between devices, shards(): lax.all_to_all(field, 'band', split_axis=1, concat_axis=0, tiled=True)  24.4 us
    all_to_all x1, waiting for transfers between devices, shards(): lax.all_to_all(orbitals.reshape(1, local_x * plane_size), 'band', split_a...  20.8 us
    all_to_all x1, blocking collectives, shards(): lax.all_to_all(partial, 'band', split_axis=0, concat_axis=0, tiled=True)  19.1 us
    ppermute x1, waiting for transfers between devices, shards(): field = keep + lax.ppermute(give, 'grid', swap)  17.9 us
    ppermute x1, waiting for transfers between devices, shards(): other = lax.ppermute(orbitals[0], 'grid', swap)  16.6 us
    all_to_all x1, starting transfers between devices, shards(): lax.all_to_all(orbitals.reshape(1, local_x * plane_size), 'band', split_a...  16.4 us
    all_to_all x1, starting transfers between devices, shards(): lax.all_to_all(field, 'band', split_axis=1, concat_axis=0, tiled=True)  10.7 us
  transfers between devices with their start and end apart: 7, of which 7 were waited for; matrix products, arithmetic and copies ran while one was open for 2% of the time, Pallas kernels for 0%

profile of v1, /device:TPU:1, one launch (start us, length us, event | category | flops | bytes accessed | tf_op | source)
XLA Modules:
  0.0 327.6 jit_solution(7174942110455836200)
XLA Ops:
  7.2 0.0 copy-start.2
  7.2 0.0 copy-start.3
  7.2 3.0 reduce.1
  10.2 2.2 all_to_all.54
  12.3 16.4 %all-to-all-start = ((f32[1,128,1458]{2,0,1:T(1,128)}), f32[1,128,1458]{2,0,1:T(1,128)S(1)}, u32[]{:S(2)}, u32[]{:S(2)}) async-start(f32[1,128,1458]{2,0,1:T(1,128)} %all_to_all.54), calls=%async_computation | async-start | bytes 1572864 | tf_op jit(solution)/shard_map/all_to_all | solution.py:43
  28.8 0.0 all-gather.3.cloned.1.call-start
  28.8 0.0 copy-done.3
  28.8 0.6 fusion.67
  33.3 20.8 %all-to-all-done = f32[1,128,1458]{2,0,1:T(1,128)S(1)} async-done(((f32[1,128,1458]{2,0,1:T(1,128)}), f32[1,128,1458]{2,0,1:T(1,128)S(1)}, u32[]{:S(2)}, u32[]{:S(2)}) %all-to-all-start) | async-done | bytes 746528 | tf_op jit(solution)/shard_map/all_to_all | solution.py:43
  54.1 0.0 copy-start
  54.1 5.7 %all_to_all.61 = f32[2,1,1458]{2,1,0:T(1,128)} all-to-all(f32[2,1,1458]{2,1,0:T(1,128)S(1)} %all_to_all.44), channel_id=1, replica_groups=mesh['band'=128,'grid'=2] {'grid'}, dimensions={0} | all-to-all | bytes 23328 | tf_op jit(solution)/shard_map/all_to_all | solution.py:49
  59.8 0.0 all-gather.3.cloned.1.call-update
  59.8 0.0 copy-done.2
  59.9 0.1 copy.42
  59.9 0.6 collective-permute-start
  60.6 1.7 concatenate.16
  62.3 0.1 broadcast_add_fusion
  62.4 16.6 %collective-permute-done = f32[36,5184]{1,0:T(8,128)S(1)} collective-permute-done((f32[36,5184]{1,0:T(8,128)S(1)}, f32[36,5184]{1,0:T(8,128)S(1)}, u32[]{:S(2)}, u32[]{:S(2)}) %collective-permute-start) | collective-permute-done | bytes 746528 | tf_op jit(solution)/shard_map/ppermute | solution.py:53
  78.9 1.7 concatenate.17
  80.6 0.0 copy-done
  80.6 80.5 %all-gather.3.cloned.1.call-done = f32[256,1,1458]{2,1,0:T(1,128)} async-done(((f32[2,1,1458]{2,1,0:T(1,128)}), f32[256,1,1458]{2,1,0:T(1,128)}) %all-gather.3.cloned.1.call-update) | async-done | bytes 1493008 | tf_op jit(solution)/shard_map/all_gather | solution.py:50
  161.1 5.2 %reduce.2 = f32[256,1458]{1,0:T(8,128)S(1)} reduce(f32[256,1,1458]{2,1,0:T(1,128)} %all-gather.3.cloned.1.call-done, f32[]{:T(128)} %constant.53), dimensions={1}, to_apply=%all-gather.reduce_sub_computation | reduce | bytes 2985988 | tf_op jit(solution)/shard_map/all_gather | solution.py:50
  166.3 1.0 reshape.135
  167.2 1.4 copy.18
  168.7 3.5 %reshape.133 = f32[72,72,72]{2,1,0:T(8,128)S(1)} reshape(f32[2,128,1458]{2,1,0:T(8,128)} %copy.18) | data formatting | bytes 2985984 | tf_op jit(solution)/shard_map/reshape | solution.py:51
  172.2 8.7 %fusion.20 = f32[72,72,72]{1,2,0:T(8,128)} fusion(f32[72,72,72]{2,1,0:T(8,128)S(1)} %reshape.133, f32[36,72,72]{2,1,0:T(8,128)} %concatenate.17, f32[36,72,72]{2,1,0:T(8,128)} %concatenate.16, pred[]{:T(512)S(6)} %eq.45, f32[72]{0:T(128)S(1)} %or_select_fusion, s32[72]{0:T(128)S(1)} %add_select_fusion.2, pred[72]{0:T(512)(128)(4,1)S(1)} %iota_compare_fusion), kind=kOutput, calls=%fused_computation.19 | convolution fusion | flops 324036288 | bytes 4479625 | tf_op jit(solution)/shard_map/by,xyz->xbz/dot_general | solution.py:60
  180.9 3.6 %copy.31 = f32[72,72,72]{2,0,1:T(8,128)} copy(f32[72,72,72]{1,2,0:T(8,128)} %fusion.20) | data formatting | bytes 2985984 | tf_op jit(solution)/shard_map/by,xyz->xbz/transpose | solution.py:60
  184.4 4.3 %fusion.38 = f32[72,72,72]{2,0,1:T(8,128)S(1)} fusion(f32[72,72,72]{2,0,1:T(8,128)} %copy.31, f32[72]{0:T(128)S(1)} %or_select_fusion, s32[72]{0:T(128)S(1)} %add_select_fusion.2, pred[72]{0:T(512)(128)(4,1)S(1)} %iota_compare_fusion), kind=kOutput, calls=%fused_computation.39 | convolution fusion | flops 322543296 | bytes 2986632 | tf_op jit(solution)/shard_map/cz,xbz->xbc/dot_general | solution.py:61
  188.7 2.7 fusion.36
  191.5 3.2 fusion.2
  194.7 5.0 %fusion.16 = f32[72,72,72]{2,1,0:T(8,128)S(1)} fusion(f32[72,72,72]{2,0,1:T(8,128)S(1)} %fusion.2, f32[72]{0:T(128)S(1)} %or_select_fusion, s32[72]{0:T(128)S(1)} %add_select_fusion.2, pred[72]{0:T(512)(128)(4,1)S(1)} %iota_compare_fusion), kind=kOutput, calls=%fused_computation.16 | convolution fusion | flops 322543296 | bytes 2986632 | tf_op jit(solution)/shard_map/by,xbz->xyz/dot_general | solution.py:64
  199.7 6.1 %multiply_multiply_fusion = f32[72,72,72]{2,1,0:T(8,128)} fusion(f32[72,72,72]{2,1,0:T(8,128)S(1)} %reshape.133, f32[72,72,72]{2,1,0:T(8,128)S(1)} %fusion.16, f32[72]{0:T(128)S(1)} %or_select_fusion, s32[72]{0:T(128)S(1)} %add_select_fusion.2, pred[72]{0:T(512)(128)(4,1)S(1)} %iota_compare_fusion), kind=kOutput, calls=%fused_computation.18 | convolution fusion | flops 323289792 | bytes 4479624 | tf_op jit(solution)/shard_map/cz,xyc->xyz/dot_general | solution.py:65
  205.8 4.4 %reshape.134 = f32[2,186624]{1,0:T(2,128)S(1)} reshape(f32[72,72,72]{2,1,0:T(8,128)} %multiply_multiply_fusion) | data formatting | bytes 2985984 | tf_op jit(solution)/shard_map/reshape | solution.py:66
  210.2 0.7 constant_dynamic-slice_fusion
  210.9 0.3 collective-permute-start.1
  211.2 0.0 copy-start.1
  211.2 17.9 %collective-permute-done.1 = f32[1,186624]{1,0:T(1,128)} collective-permute-done((f32[1,186624]{1,0:T(1,128)S(1)}, f32[1,186624]{1,0:T(1,128)}, u32[]{:S(2)}, u32[]{:S(2)}) %collective-permute-start.1) | collective-permute-done | bytes 746528 | tf_op jit(solution)/shard_map/ppermute | solution.py:69
  229.1 8.9 %add_reduce_fusion = f32[186624]{0:T(1024)S(1)} fusion(f32[1,186624]{1,0:T(1,128)} %collective-permute-done.1, f32[2,186624]{1,0:T(2,128)S(1)} %reshape.134, s32[]{:T(128)S(6)} %select_n.119), kind=kLoop, calls=%fused_computation.31 | loop fusion | flops 186624 | bytes 2239492 | tf_op jit(solution)/shard_map/add | solution.py:69
  238.0 1.9 all_to_all.55
  239.9 10.7 %all-to-all-start.2 = ((f32[1,128,1458]{2,0,1:T(1,128)}), f32[1,128,1458]{2,0,1:T(1,128)S(1)}, u32[]{:S(2)}, u32[]{:S(2)}) async-start(f32[1,128,1458]{2,0,1:T(1,128)} %all_to_all.55), calls=%async_computation.2 | async-start | bytes 1572864 | tf_op jit(solution)/shard_map/all_to_all | solution.py:71
  250.6 0.0 copy-done.1
  250.7 0.9 copy.27
  251.6 24.4 %all-to-all-done.2 = f32[1,128,1458]{2,0,1:T(1,128)S(1)} async-done(((f32[1,128,1458]{2,0,1:T(1,128)}), f32[1,128,1458]{2,0,1:T(1,128)S(1)}, u32[]{:S(2)}, u32[]{:S(2)}) %all-to-all-start.2) | async-done | bytes 746528 | tf_op jit(solution)/shard_map/all_to_all | solution.py:71
  276.0 0.9 copy.26
  276.9 1.5 fusion.29
  278.4 0.1 copy.28
  278.5 19.1 %all_to_all.62 = f32[128,1,128]{2,1,0:T(1,128)S(1)} all-to-all(f32[128,1,128]{2,1,0:T(1,128)S(1)} %copy.28), channel_id=1, replica_groups=mesh['band'=128,'grid'=2] {'band'}, dimensions={0} | all-to-all | bytes 131072 | tf_op jit(solution)/shard_map/all_to_all | solution.py:75
  297.5 0.2 reduce_sum.9
  297.7 0.3 collective-permute-start.2
  298.0 2.2 collective-permute-done.2
  300.1 0.7 broadcast_in_dim.52
  300.8 6.9 %all-to-all-start.4 = ((f32[128,1,128]{2,1,0:T(1,128)}), f32[128,1,128]{2,1,0:T(1,128)S(1)}, u32[]{:S(2)}, u32[]{:S(2)}) async-start(f32[128,1,128]{2,1,0:T(1,128)} %broadcast_in_dim.52), calls=%async_computation.4 | async-start | bytes 131072 | tf_op jit(solution)/shard_map/all_to_all | solution.py:78
  307.7 1.9 copy.29
  309.6 10.3 %all-to-all-done.4 = f32[128,1,128]{2,1,0:T(1,128)S(1)} async-done(((f32[128,1,128]{2,1,0:T(1,128)}), f32[128,1,128]{2,1,0:T(1,128)S(1)}, u32[]{:S(2)}, u32[]{:S(2)}) %all-to-all-start.4) | async-done | bytes 65568 | tf_op jit(solution)/shard_map/all_to_all | solution.py:78
  319.9 0.6 copy.44
  (8 shorter events, 0.1 us)
Async XLA Ops:
  7.2 52.7 %copy-start.2 = (f32[1,36,5184]{2,0,1:T(1,128)S(1)}, f32[1,36,5184]{2,0,1:T(1,128)}, u32[]{:S(2)}) copy-start(f32[1,36,5184]{2,0,1:T(1,128)} %param.2) | copy-start | bytes 2239492
  7.2 21.6 %copy-start.3 = (s32[128]{0:T(128)S(1)}, s32[128]{0:T(128)}, u32[]{:S(2)}) copy-start(s32[128]{0:T(128)} %param.3) | copy-start | bytes 1540
  12.3 41.7 %all-to-all-start = ((f32[1,128,1458]{2,0,1:T(1,128)}), f32[1,128,1458]{2,0,1:T(1,128)S(1)}, u32[]{:S(2)}, u32[]{:S(2)}) async-start(f32[1,128,1458]{2,0,1:T(1,128)} %all_to_all.54), calls=%async_computation | async-start | bytes 1572864 | tf_op jit(solution)/shard_map/all_to_all | solution.py:43
  28.8 132.3 %all-gather.3.cloned.1.call-start = ((), (), s32[]{:S(2)}) async-start(), calls=%async_computation.5 | async-start | bytes 1585152 | tf_op jit(solution)/shard_map/all_gather | solution.py:50
  54.1 26.6 %copy-start = (f32[1,128,1458]{2,0,1:T(1,128)}, f32[1,128,1458]{2,0,1:T(1,128)S(1)}, u32[]{:S(2)}) copy-start(f32[1,128,1458]{2,0,1:T(1,128)S(1)} %all-to-all-done) | copy-start | bytes 2239492
  59.9 19.0 %collective-permute-start = (f32[36,5184]{1,0:T(8,128)S(1)}, f32[36,5184]{1,0:T(8,128)S(1)}, u32[]{:S(2)}, u32[]{:S(2)}) collective-permute-start(f32[36,5184]{1,0:T(8,128)S(1)} %bitcast.49), channel_id=1, source_target_pairs={{0,1},{1,0},{2,3},{3,2},{4,5},{5,4},{6,7},{7,6},{8,9},{9,8},{10,11... | collective-permute-start | bytes 2239496 | tf_op jit(solution)/shard_map/ppermute | solution.py:53
  210.9 18.3 %collective-permute-start.1 = (f32[1,186624]{1,0:T(1,128)S(1)}, f32[1,186624]{1,0:T(1,128)}, u32[]{:S(2)}, u32[]{:S(2)}) collective-permute-start(f32[1,186624]{1,0:T(1,128)S(1)} %constant_dynamic-slice_fusion), channel_id=1, source_target_pairs={{0,1},{1,0},{2,3},{3,2},{4,5},{5,4},{6,7},{7,6},{8,9},{9,8},{10,11... | collective-permute-start | bytes 2239496 | tf_op jit(solution)/shard_map/ppermute | solution.py:69
  211.2 39.4 %copy-start.1 = (f32[1,128,1458]{2,0,1:T(1,128)S(1)}, f32[1,128,1458]{2,0,1:T(1,128)}, u32[]{:S(2)}) copy-start(f32[1,128,1458]{2,0,1:T(1,128)} %copy-done) | copy-start | bytes 2239492
  239.9 36.0 %all-to-all-start.2 = ((f32[1,128,1458]{2,0,1:T(1,128)}), f32[1,128,1458]{2,0,1:T(1,128)S(1)}, u32[]{:S(2)}, u32[]{:S(2)}) async-start(f32[1,128,1458]{2,0,1:T(1,128)} %all_to_all.55), calls=%async_computation.2 | async-start | bytes 1572864 | tf_op jit(solution)/shard_map/all_to_all | solution.py:71
  297.7 2.5 collective-permute-start.2
  300.8 19.1 %all-to-all-start.4 = ((f32[128,1,128]{2,1,0:T(1,128)}), f32[128,1,128]{2,1,0:T(1,128)S(1)}, u32[]{:S(2)}, u32[]{:S(2)}) async-start(f32[128,1,128]{2,1,0:T(1,128)} %broadcast_in_dim.52), calls=%async_computation.4 | async-start | bytes 131072 | tf_op jit(solution)/shard_map/all_to_all | solution.py:78
Sparse Core Ops, SparseCore 0:
  60.0 101.0 all-gather.2

commit v2 on v1

v2 whole, which is shorter than its diff:
```python
import functools
import math

import jax
import jax.numpy as jnp
import numpy as np
from jax import lax
from jax.experimental import pallas as pl
from jax.experimental.pallas import tpu as pltpu
from jax.sharding import PartitionSpec as P

N = 72
PAD = 80
BF = jnp.bfloat16
F32 = jnp.float32

def tables():
    pos = np.arange(N)
    half = N // 2
    freq = np.where(pos <= half, pos, pos - half)
    ang = (freq[:, None] * pos[None, :] % N) * (2.0 * math.pi / N)
    w = np.where((pos == 0) | (pos == half), 1.0 / math.sqrt(N), math.sqrt(2.0 / N))
    basis = np.where((pos <= half)[:, None], np.cos(ang), np.sin(ang)) * w[:, None]
    sq = (freq * (2.0 * math.pi / N)) ** 2

    def split(t):
        hi = jnp.asarray(t, F32).astype(BF)
        lo = (jnp.asarray(t, F32) - hi.astype(F32)).astype(BF)
        return hi, lo

    def left(t):
        hi, lo = split(t)
        put = lambda a: jnp.pad(a, ((0, PAD - N), (0, PAD - N)))
        return jnp.concatenate([put(hi), put(hi), put(lo)], axis=1)

    def right(t):
        hi, lo = split(t)
        put = lambda a: jnp.pad(a, ((0, 128 - N), (0, 128 - N)))
        top = jnp.concatenate([put(hi), put(lo)], axis=1)
        low = jnp.concatenate([put(hi), jnp.zeros((128, 128), BF)], axis=1)
        return jnp.concatenate([top, low], axis=0)

    sq_rows = np.zeros((PAD, 128), np.float32); sq_rows[:N] = sq[:, None]
    sq_pair = np.zeros((N, 128), np.float32); sq_pair[:, :N] = sq[:, None] + sq[None, :]
    return (left(basis), left(basis.T), right(basis.T), right(basis), jnp.asarray(sq_rows), jnp.asarray(sq_pair))


def halves(v):
    hi = v.astype(BF)
    lo = (v - hi.astype(F32)).astype(BF)
    return hi, lo


def left_dot(table, planes):
    cols = []
    for v in planes:
        hi, lo = halves(v)
        cols.append(jnp.concatenate([hi, lo, hi], axis=0))
    out = jnp.dot(table, jnp.concatenate(cols, axis=1), preferred_element_type=F32)
    return [out[:, 128 * i : 128 * i + 128] for i in range(len(planes))]


def right_dot(v, table):
    hi, lo = halves(v)
    out = jnp.dot(jnp.concatenate([hi, lo], axis=1), table, preferred_element_type=F32)
    return out[:, :128] + out[:, 128:]


def pad_rows(v):
    return jnp.concatenate([v, jnp.zeros((PAD - N, 128), F32)], axis=0)


def convolve(own, lent, work, tl, til, tr, tir, sq_rows, sq_pair, UA, UB, UC):
    lane = lax.broadcasted_iota(jnp.int32, (1, 128), 1) < N

    def stage_a(step, carry):
        for u in range(UA):
            base = pl.multiple_of((step * UA + u) * 2 * N, 8)
            rows = pl.ds(base, 2 * N)
            d = jnp.where(lane, own[rows, :] * lent[rows, :], 0.0)
            z = right_dot(d, tr[...])
            a, b = left_dot(tl[...], [pad_rows(z[:N]), pad_rows(z[N:])])
            work[rows, :] = jnp.concatenate([a[:N], b[:N]], axis=0)
        return carry

    lax.fori_loop(0, 36 // UA, stage_a, 0)

    def stage_b(step, carry):
        for u in range(UB):
            b = (step * UB + u) * 2
            planes = [pad_rows(work[pl.ds(b + i, N, stride=N), :]) for i in range(2)]
            planes = left_dot(tl[...], planes)
            for i in range(2):
                total = sq_rows[...] + sq_pair[pl.ds(b + i, 1), :]
                positive = total > 0
                kern = jnp.where(positive, (-0.25 * math.pi) / jnp.where(positive, total, 1.0), 0.0)
                planes[i] = planes[i] * kern
            planes = left_dot(til[...], planes)
            for i in range(2):
                work[pl.ds(b + i, N, stride=N), :] = planes[i][:N]
        return carry

    lax.fori_loop(0, 36 // UB, stage_b, 0)

    def stage_c(step, carry):
        for u in range(UC):
            base = pl.multiple_of((step * UC + u) * 2 * N, 8)
            rows = pl.ds(base, 2 * N)
            v = work[rows, :]
            a, b = left_dot(til[...], [pad_rows(v[:N]), pad_rows(v[N:])])
            z = right_dot(jnp.concatenate([a[:N], b[:N]], axis=0), tir[...])
            own[rows, :] = z * lent[rows, :]
        return carry

    lax.fori_loop(0, 36 // UC, stage_c, 0)


def from_plane(ref, dst, slab):
    for y in range(N):
        dst[pl.ds(slab * 2592 + y, 36, stride=N), :N] = ref[:, N * y : N * y + N]


def spans():
    for j in range(81):
        first, at = divmod(N * j, 1458)
        fit = min(N, 1458 - at)
        yield j, first, at, fit


def from_blocks(ref, dst, slab):
    for j, first, at, fit in spans():
        rows = pl.ds(slab * 2592 + j, 32, stride=81)
        v = ref[first, :, at : at + fit]
        if fit < N:
            v = jnp.concatenate([v, ref[first + 1, :, : N - fit]], axis=1)
        dst[rows, :N] = v


def to_blocks(src, ref, slab):
    for j, first, at, fit in spans():
        v = src[pl.ds(slab * 2592 + j, 32, stride=81), :]
        ref[first, :, at : at + fit] = v[:, :fit]
        if fit < N:
            ref[first + 1, :, : N - fit] = v[:, fit:N]


def fft_kernel(U, mine, other, lent_in, tl, til, tr, tir, sq_rows, sq_pair, out, own, lent, work):
    from_plane(mine, own, 0)
    from_plane(other, own, 1)
    for s in range(2):
        from_blocks(lent_in.at[s], lent, s)
    convolve(own, lent, work, tl, til, tr, tir, sq_rows, sq_pair, *U)
    for s in range(2):
        to_blocks(own, out.at[s], s)


def fft_call(mine, other, lent, U=(9, 9, 9)):
    vm = pl.BlockSpec(memory_space=pltpu.VMEM)
    return pl.pallas_call(
        functools.partial(fft_kernel, U),
        out_shape=jax.ShapeDtypeStruct((2, 4, 32, 1458), F32),
        in_specs=[vm] * 9,
        out_specs=vm,
        scratch_shapes=[pltpu.VMEM((5184, 128), F32) for _ in range(3)],
        compiler_params=pltpu.CompilerParams(vmem_limit_bytes=48 << 20),
    )(mine, other, lent, *tables())


MESH = pl.DeviceIdType.MESH
BANDS = 128
CELLS = 1458


def send(src, dst, send_sem, recv_sem, device):
    return pltpu.make_async_remote_copy(
        src_ref=src, dst_ref=dst, send_sem=send_sem, recv_sem=recv_sem, device_id=device, device_id_type=MESH
    )


def greet(barrier, device):
    pl.semaphore_signal(barrier, inc=1, device_id=device, device_id_type=MESH)


def greet_bands(barrier, band):
    def one(k, carry):
        greet(barrier, {"band": lax.rem(band + k, BANDS)})
        return carry

    lax.fori_loop(1, BANDS, one, 0)


def lend_kernel(
    owners, orb, cols, other, lent, rows, blocks, picked,
    a2a_send, a2a_recv, own_sem, swap_send, swap_recv, ag_send, ag_recv,
):
    band, grid = lax.axis_index("band"), lax.axis_index("grid")
    partner = {"grid": 1 - grid}
    barrier = pltpu.get_barrier_semaphore()
    greet_bands(barrier, band)
    greet(barrier, partner)
    from_plane(orb, rows, 0)
    to_blocks(rows, blocks, 0)
    pl.semaphore_wait(barrier, BANDS)

    def block(c):
        return blocks.at[lax.rem(c, 4), pl.ds(lax.div(c, 4), 1), :]

    def a2a(to, slot):
        return send(block(to), cols.at[pl.ds(slot, 1), :], a2a_send.at[to], a2a_recv.at[slot], {"band": to})

    def start(k, carry):
        a2a(lax.rem(band + k, BANDS), band).start()
        return carry

    lax.fori_loop(1, BANDS, start, 0)
    own = pltpu.make_async_copy(block(band), cols.at[pl.ds(band, 1), :], own_sem)
    own.start()
    whole = send(orb, other, swap_send.at[0], swap_recv.at[0], partner)
    whole.start()

    def finish(k, carry):
        c = lax.rem(band + k, BANDS)
        a2a(c, c).wait_recv()
        return carry

    lax.fori_loop(1, BANDS, finish, 0)
    own.wait()

    core, z = lax.rem(band, 2), lax.rem(lax.div(band, 2), 8)
    xy = lax.div(band, 16)
    xh, y = lax.div(xy, 4), lax.rem(xy, 4)
    pick_mine, pick_other = owners[grid], owners[1 - grid]
    picked[0:1, :] = cols[pl.ds(pick_mine, 1), :]
    picked[1:2, :] = cols[pl.ds(pick_other, 1), :]

    def at(xy_, z_):
        return pl.ds(4 * xy_ + lax.div(z_, 2), 1)

    zlo = lax.rem(z, 2)
    keep = pltpu.make_async_copy(picked.at[pl.ds(0, 1), :], lent.at[0, zlo, core, at(xy, z), :], own_sem)
    keep.start()
    give = send(
        picked.at[pl.ds(1, 1), :], lent.at[1, zlo, core, at(xy, z), :], swap_send.at[1], swap_recv.at[1], partner
    )
    give.start()
    keep.wait()
    give.wait_recv()

    def device(xh_, y_, z_, core_):
        return {"band": ((xh_ * 4 + y_) * 8 + z_) * 2 + core_}

    started = []

    def along_z(d, z_, to):
        part = lent.at[:, lax.rem(z_, 2), core, at(xy, z_), :]
        return send(part, part, ag_send.at[d - 1], ag_recv.at[d - 1], device(xh, y, to, core))

    for d in range(1, 8):
        c = along_z(d, z, lax.rem(z + d, 8))
        c.start()
        started.append(c)
    for d in range(1, 8):
        along_z(d, lax.rem(z + 8 - d, 8), z).wait_recv()

    def column(xh_, y_):
        return lent.at[:, :, core, pl.ds(16 * xh_ + 4 * y_, 4), :]

    def copy(part, slot, to):
        return send(part, part, ag_send.at[slot], ag_recv.at[slot], to)

    c = copy(column(xh, y), 7, device(1 - xh, y, z, core))
    c.start()
    started.append(c)
    for d in range(1, 4):
        c = copy(column(xh, y), 7 + d, device(xh, lax.rem(y + d, 4), z, core))
        c.start()
        started.append(c)
    copy(column(1 - xh, y), 7, device(1 - xh, y, z, core)).wait_recv()
    for d in range(1, 4):
        c = copy(column(1 - xh, y), 10 + d, device(xh, lax.rem(y + d, 4), z, core))
        c.start()
        started.append(c)

    def half(xh_, core_):
        return lent.at[:, :, core_, pl.ds(16 * xh_, 16), :]

    for n, x_ in ((7, xh), (10, 1 - xh)):
        for d in range(1, 4):
            copy(column(x_, lax.rem(y + 4 - d, 4)), n + d, device(xh, y, z, core)).wait_recv()
        c = send(half(x_, core), half(x_, core), ag_send.at[n // 3 + 12], ag_recv.at[n // 3 + 12], device(xh, y, z, 1 - core))
        c.start()
        started.append(c)
    for n, x_ in ((7, xh), (10, 1 - xh)):
        send(half(x_, 1 - core), half(x_, 1 - core), ag_send.at[n // 3 + 12], ag_recv.at[n // 3 + 12], device(xh, y, z, core)).wait_recv()
    for c in started:
        c.wait_send()
    whole.wait()
    give.wait_send()

    def sent(k, carry):
        a2a(lax.rem(band + k, BANDS), band).wait_send()
        return carry

    lax.fori_loop(1, BANDS, sent, 0)


def lend_call(owners, orb):
    vm = pl.BlockSpec(memory_space=pltpu.VMEM)
    dma = pltpu.SemaphoreType.DMA
    return pl.pallas_call(
        lend_kernel,
        out_shape=(
            jax.ShapeDtypeStruct((BANDS, CELLS), F32),
            jax.ShapeDtypeStruct((36, 5184), F32),
            jax.ShapeDtypeStruct((2, 2, 2, 32, CELLS), F32),
        ),
        in_specs=[pl.BlockSpec(memory_space=pltpu.SMEM), vm],
        out_specs=(vm, vm, vm),
        scratch_shapes=[
            pltpu.VMEM((2592, 128), F32), pltpu.VMEM((4, 32, CELLS), F32), pltpu.VMEM((2, CELLS), F32),
            dma((BANDS,)), dma((BANDS,)), dma, dma((2,)), dma((2,)), dma((16,)), dma((16,)),
        ],
        compiler_params=pltpu.CompilerParams(collective_id=0, has_side_effects=True, vmem_limit_bytes=32 << 20),
    )(owners, orb)


def matrix_kernel(
    part, cols, field, matrix, summed, arrived, product, first, second,
    a2a_send, a2a_recv, own_sem, swap_send, swap_recv, m_send, m_recv,
):
    band, grid = lax.axis_index("band"), lax.axis_index("grid")
    xy, t = lax.div(band, 16), lax.rem(band, 16)
    barrier = pltpu.get_barrier_semaphore()
    greet_bands(barrier, band)
    for k in range(8):
        greet(barrier, {"band": 16 * lax.rem(xy + k, 8) + t, "grid": 1 - grid})
    pl.semaphore_wait(barrier, BANDS - 1 + 8)
    mine = lax.div(band, 32)

    def octet(k):
        return pl.ds(pl.multiple_of(8 * lax.rem(mine + k, 4), 8), 8)

    def swap(k):
        return send(
            part.at[1, :, octet(k), :], arrived.at[:, octet(k), :], swap_send.at[k], swap_recv.at[k], {"grid": 1 - grid}
        )

    for k in range(4):
        swap(k).start()

    def a2a(to, slot):
        return send(
            summed.at[lax.rem(to, 4), pl.ds(lax.div(to, 4), 1), :],
            field.at[pl.ds(slot, 1), :],
            a2a_send.at[to], a2a_recv.at[slot], {"band": to},
        )

    own = pltpu.make_async_copy(
        summed.at[lax.rem(band, 4), pl.ds(lax.div(band, 4), 1), :], field.at[pl.ds(band, 1), :], own_sem
    )
    for k in range(4):
        swap(k).wait_recv()
        rows = octet(k)
        summed[:, rows, :] = part[0, :, rows, :] + arrived[:, rows, :]

        def start(n, carry):
            to = 32 * lax.rem(mine + k, 4) + lax.rem(band + n, 32)
            a2a(to, band).start()
            return carry

        if k == 0:
            own.start()
        lax.fori_loop(1 if k == 0 else 0, 32, start, 0)

    def finish(k, carry):
        c = lax.rem(band + k, BANDS)
        a2a(c, c).wait_recv()
        return carry

    lax.fori_loop(1, BANDS, finish, 0)
    own.wait()
    oh, ol = halves(cols[...])
    fh, fl = halves(field[...])
    dot = lambda a, b: lax.dot_general(a, b, (((1,), (1,)), ((), ())), preferred_element_type=F32)
    product[...] = ((dot(oh, fl) + dot(ol, fh)) + dot(oh, fh)) * (1.0 / 373248.0)

    def block(c):
        return pl.ds(pl.multiple_of(8 * c, 8), 8)

    def scatter(k, to, slot):
        return send(
            product.at[block(to), :], first.at[slot], m_send.at[k], m_recv.at[k], {"band": 16 * xy + to}
        )

    for k in range(1, 16):
        scatter(k, lax.rem(t + k, 16), t).start()
    first[t] = product[block(t), :]
    for k in range(1, 16):
        scatter(k, t, lax.rem(t + 16 - k, 16)).wait_recv()
    total = first[0]
    for k in range(1, 16):
        total = total + first[k]
    where = 2 * xy + grid
    second[where] = total

    def across(k):
        q, g = k // 2, lax.rem(grid + k, 2)
        return lax.rem(xy + q, 8), g

    def share(k, slot, to):
        return send(second.at[slot], second.at[slot], m_send.at[15 + k], m_recv.at[15 + k], to)

    for k in range(1, 16):
        x_, g_ = across(k)
        share(k, where, {"band": 16 * x_ + t, "grid": g_}).start()
    for k in range(1, 16):
        x_, g_ = lax.rem(xy + 8 - k // 2, 8), lax.rem(grid + k, 2)
        share(k, 2 * x_ + g_, {"band": 16 * x_ + t, "grid": g_}).wait_recv()
    total = second[0]
    for k in range(1, 16):
        total = total + second[k]
    matrix[block(t), :] = total

    def spread(k, to, slot):
        return send(
            matrix.at[block(slot), :], matrix.at[block(slot), :], m_send.at[30 + k], m_recv.at[30 + k],
            {"band": 16 * xy + to},
        )

    for k in range(1, 16):
        spread(k, lax.rem(t + k, 16), t).start()
    for k in range(1, 16):
        spread(k, t, lax.rem(t + 16 - k, 16)).wait_recv()
    for k in range(4):
        swap(k).wait_send()
    for k in range(1, 16):
        scatter(k, lax.rem(t + k, 16), t).wait_send()
        share(k, where, {"grid": 1 - grid}).wait_send()
        spread(k, lax.rem(t + k, 16), t).wait_send()

    def sent(k, carry):
        a2a(lax.rem(band + k, BANDS), band).wait_send()
        return carry

    lax.fori_loop(1, BANDS, sent, 0)


def matrix_call(part, cols):
    vm = pl.BlockSpec(memory_space=pltpu.VMEM)
    dma = pltpu.SemaphoreType.DMA
    return pl.pallas_call(
        matrix_kernel,
        out_shape=(
            jax.ShapeDtypeStruct((BANDS, CELLS), F32),
            jax.ShapeDtypeStruct((BANDS, BANDS), F32),
        ),
        in_specs=[vm, vm],
        out_specs=(vm, vm),
        scratch_shapes=[
            pltpu.VMEM((4, 32, CELLS), F32), pltpu.VMEM((4, 32, CELLS), F32), pltpu.VMEM((BANDS, BANDS), F32),
            pltpu.VMEM((16, 8, BANDS), F32), pltpu.VMEM((16, 8, BANDS), F32),
            dma((BANDS,)), dma((BANDS,)), dma, dma((4,)), dma((4,)), dma((46,)), dma((46,)),
        ],
        compiler_params=pltpu.CompilerParams(collective_id=1, has_side_effects=True, vmem_limit_bytes=32 << 20),
    )(part, cols)


def shards(orbitals, owners):
    mine = orbitals[0]
    cols, other, lent = lend_call(owners, mine)
    part = fft_call(mine, other, lent.reshape(2, 4, 32, CELLS))
    field, matrix = matrix_call(part, cols)
    return (field[None], matrix)


def solution(mesh):
    in_specs = (P("band", "grid", None), P())
    out_specs = (P("grid", None, "band"), P())
    return jax.shard_map(shards, mesh=mesh, in_specs=in_specs, out_specs=out_specs, check_vma=False)
```

time: 333 us -> 146 us (0.44); the launches traced: 328 us -> 146 us
  waiting for transfers between devices: 173 us -> 0 us
  Pallas kernels: 0 us -> 141 us
  starting transfers between devices: 35.3 us -> 0 us
  matrix products: 31.5 us -> 0 us
  blocking collectives: 24.8 us -> 0 us
  local copies, waits for them, and re-layouts: 27.9 us -> 3.71 us
  between operations: 18.3 us -> 0.77 us
  other arithmetic: 17.3 us -> 0 us
    pallas_call x0 -> x3, Pallas kernels: none -> 141 us  [the longest x1 63.8 us: lend_call(): pl.pallas_call(lend_kernel, out_shape=(jax.ShapeDtypeStruct((BANDS, CELLS...]
    all_gather x1 -> x0, waiting for transfers between devices: 80.5 us -> none  [shards(): lent = lax.all_gather(picked, 'band', axis=0, tiled=False)]
    all_to_all x3 -> x0, waiting for transfers between devices: 55.4 us -> none  [the longest x1 24.4 us: shards(): lax.all_to_all(field, 'band', split_axis=1, concat_axis=0, tiled=True)]
    ppermute x3 -> x0, waiting for transfers between devices: 36.6 us -> none  [the longest x1 17.9 us: shards(): field = keep + lax.ppermute(give, 'grid', swap)]
    all_to_all x3 -> x0, starting transfers between devices: 34 us -> none  [the longest x1 16.4 us: shards(): lax.all_to_all(orbitals.reshape(1, local_x * plane_size), 'band', split_a...]
    dot_general x7 -> x0, matrix products: 31.5 us -> none  [the longest x1 8.68 us: shards(): jnp.einsum('by,xyz->xbz', table, values, precision=HIGHEST_PRECISION)]
    all_to_all x2 -> x0, blocking collectives: 24.8 us -> none  [the longest x1 19.1 us: shards(): lax.all_to_all(partial, 'band', split_axis=0, concat_axis=0, tiled=True)]
    add x3 -> x0, other arithmetic: 8.94 us -> none  [the longest x1 8.87 us: shards(): field = keep + lax.ppermute(give, 'grid', swap)]
  transfers between devices with their start and end apart: 7 -> 0, of which waited for: 7 -> 0; matrix products, arithmetic and copies ran while one was open for 2% -> 0% of each run, Pallas kernels for 0% -> 0%
where the time goes in v2:
time: 146 us
  Pallas kernels  141 us (97%)
  local copies, waits for them, and re-layouts  3.71 us (3%)
    pallas_call x1, Pallas kernels, lend_call(): pl.pallas_call(lend_kernel, out_shape=(jax.ShapeDtypeStruct((BANDS, CELLS...  63.8 us
    pallas_call x1, Pallas kernels, matrix_call(): pl.pallas_call(matrix_kernel, out_shape=(jax.ShapeDtypeStruct((BANDS, CEL...  63 us
    pallas_call x1, Pallas kernels, fft_call(): pl.pallas_call(functools.partial(fft_kernel, U), out_shape=jax.ShapeDtype...  14.3 us
    unnamed x17, local copies, waits for them, and re-layouts  3.71 us

profile of v2, /device:TPU:1, one launch (start us, length us, event | category | flops | bytes accessed | tf_op | source)
XLA Modules:
  0.0 145.6 jit_solution(12109886693901513485)
XLA Ops:
  0.6 0.0 copy-start
  0.6 0.0 copy-start.1
  0.7 0.0 copy-start.2
  0.7 0.0 copy-start.3
  0.7 0.0 copy-start.5
  0.7 0.0 copy-start.4
  0.7 0.0 copy-start.6
  0.7 1.3 copy.17
  2.0 0.0 copy-done.6
  2.0 63.8 %shard_map.131 = (f32[128,1458]{1,0:T(8,128)S(1)}, f32[36,5184]{1,0:T(8,128)S(1)}, f32[2,2,2,32,1458]{4,3,2,1,0:T(8,128)S(1)}) custom-call(s32[128]{0:T(128)S(1)} %copy-done.6, f32[36,5184]{1,0:T(8,128)S(1)} %bitcast.5), custom_call_target="tpu_custom_call" | custom-call | tf_op jit(solution)/shard_map/pallas_call | solution.py:310
  65.9 0.0 copy-done
  65.9 0.0 copy-done.1
  65.9 0.0 copy-done.2
  65.9 0.0 copy-done.3
  65.9 0.0 copy-done.5
  65.9 0.0 copy-done.4
  65.9 14.3 %shard_map.132.part = f32[2,4,32,1458]{3,2,1,0:T(8,128)S(1)} custom-call(f32[36,5184]{1,0:T(8,128)S(1)} %bitcast.6, f32[36,5184]{1,0:T(8,128)S(1)} %get-tuple-element.7.other, f32[2,4,32,1458]{3,2,1,0:T(8,128)S(1)} %bitcast.7, bf16[80,240]{1,0:T(8,128)(2,1)S(1)} %copy-done.3, bf16[80,240]{1,0:T(8,128)(2,1)S(1)} %copy-done.2, bf16[256,256]{1,0:T(8,128)(2,1)S(1)} %copy-done.1, ...), custom_call_target="tpu_custom_call" | custom-call | tf_op jit(solution)/shard_map/pallas_call | solution.py:159
  80.2 63.0 %shard_map.133 = (f32[128,1458]{1,0:T(8,128)S(1)}, f32[128,128]{1,0:T(8,128)S(1)}) custom-call(f32[2,4,32,1458]{3,2,1,0:T(8,128)S(1)} %shard_map.132.part, f32[128,1458]{1,0:T(8,128)S(1)} %get-tuple-element.9.cols), custom_call_target="tpu_custom_call" | custom-call | tf_op jit(solution)/shard_map/pallas_call | solution.py:451
  143.2 1.7 %copy.14 = f32[1,128,1458]{1,0,2:T(1,128)} copy(f32[1,128,1458]{2,1,0:T(8,128)S(1)} %bitcast.8) | data formatting | bytes 1492992
  144.9 0.6 copy.19
Async XLA Ops:
  0.6 65.2 %copy-start = (bf16[256,256]{1,0:T(8,128)(2,1)S(1)}, bf16[256,256]{1,0:T(8,128)(2,1)}, u32[]{:S(2)}) copy-start(bf16[256,256]{1,0:T(8,128)(2,1)} %constant.60.tir) | copy-start | bytes 393220
  0.6 65.2 %copy-start.1 = (bf16[256,256]{1,0:T(8,128)(2,1)S(1)}, bf16[256,256]{1,0:T(8,128)(2,1)}, u32[]{:S(2)}) copy-start(bf16[256,256]{1,0:T(8,128)(2,1)} %constant.55.tr) | copy-start | bytes 393220
  0.7 65.2 %copy-start.2 = (bf16[80,240]{1,0:T(8,128)(2,1)S(1)}, bf16[80,240]{1,0:T(8,128)(2,1)}, u32[]{:S(2)}) copy-start(bf16[80,240]{1,0:T(8,128)(2,1)} %constant.50.til) | copy-start | bytes 115204
  0.7 65.2 %copy-start.3 = (bf16[80,240]{1,0:T(8,128)(2,1)S(1)}, bf16[80,240]{1,0:T(8,128)(2,1)}, u32[]{:S(2)}) copy-start(bf16[80,240]{1,0:T(8,128)(2,1)} %constant.43.tl) | copy-start | bytes 115204
  0.7 65.2 %copy-start.5 = (f32[72,128]{1,0:T(8,128)S(1)}, f32[72,128]{1,0:T(8,128)}, u32[]{:S(2)}) copy-start(f32[72,128]{1,0:T(8,128)} %constant.15.clone.sq_pair) | copy-start | bytes 110596
  0.7 65.2 %copy-start.4 = (f32[80,128]{1,0:T(8,128)S(1)}, f32[80,128]{1,0:T(8,128)}, u32[]{:S(2)}) copy-start(f32[80,128]{1,0:T(8,128)} %constant.14.clone.sq_rows) | copy-start | bytes 122884
  0.7 1.3 copy-start.6

commit v3 on v2

v3 whole, which is shorter than its diff:
```python
import functools
import math

import jax
import jax.numpy as jnp
import numpy as np
from jax import lax
from jax.experimental import pallas as pl
from jax.experimental.pallas import tpu as pltpu
from jax.sharding import PartitionSpec as P

N = 72
PAD = 80
BF = jnp.bfloat16
F32 = jnp.float32

def tables():
    pos = np.arange(N)
    half = N // 2
    freq = np.where(pos <= half, pos, pos - half)
    ang = (freq[:, None] * pos[None, :] % N) * (2.0 * math.pi / N)
    w = np.where((pos == 0) | (pos == half), 1.0 / math.sqrt(N), math.sqrt(2.0 / N))
    basis = np.where((pos <= half)[:, None], np.cos(ang), np.sin(ang)) * w[:, None]
    sq = (freq * (2.0 * math.pi / N)) ** 2

    def split(t):
        hi = jnp.asarray(t, F32).astype(BF)
        lo = (jnp.asarray(t, F32) - hi.astype(F32)).astype(BF)
        return hi, lo

    def left(t):
        hi, lo = split(t)
        put = lambda a: jnp.pad(a, ((0, PAD - N), (0, PAD - N)))
        return jnp.concatenate([put(hi), put(hi), put(lo)], axis=1)

    def right(t):
        hi, lo = split(t)
        put = lambda a: jnp.pad(a, ((0, 128 - N), (0, 128 - N)))
        top = jnp.concatenate([put(hi), put(lo)], axis=1)
        low = jnp.concatenate([put(hi), jnp.zeros((128, 128), BF)], axis=1)
        return jnp.concatenate([top, low], axis=0)

    sq_rows = np.zeros((PAD, 128), np.float32); sq_rows[:N] = sq[:, None]
    sq_pair = np.zeros((N, 128), np.float32); sq_pair[:, :N] = sq[:, None] + sq[None, :]
    return (left(basis), left(basis.T), right(basis.T), right(basis), jnp.asarray(sq_rows), jnp.asarray(sq_pair))


def halves(v):
    hi = v.astype(BF)
    lo = (v - hi.astype(F32)).astype(BF)
    return hi, lo


def left_dot(table, planes):
    cols = []
    for v in planes:
        hi, lo = halves(v)
        cols.append(jnp.concatenate([hi, lo, hi], axis=0))
    out = jnp.dot(table, jnp.concatenate(cols, axis=1), preferred_element_type=F32)
    return [out[:, 128 * i : 128 * i + 128] for i in range(len(planes))]


def right_dot(v, table):
    hi, lo = halves(v)
    out = jnp.dot(jnp.concatenate([hi, lo], axis=1), table, preferred_element_type=F32)
    return out[:, :128] + out[:, 128:]


def pad_rows(v):
    return jnp.concatenate([v, jnp.zeros((PAD - N, 128), F32)], axis=0)


def convolve(own, lent, work, tl, til, tr, tir, sq_rows, sq_pair, UA, UB, UC):
    lane = lax.broadcasted_iota(jnp.int32, (1, 128), 1) < N

    def stage_a(step, carry):
        for u in range(UA):
            base = pl.multiple_of((step * UA + u) * 2 * N, 8)
            rows = pl.ds(base, 2 * N)
            d = jnp.where(lane, own[rows, :] * lent[rows, :], 0.0)
            z = right_dot(d, tr[...])
            a, b = left_dot(tl[...], [pad_rows(z[:N]), pad_rows(z[N:])])
            work[rows, :] = jnp.concatenate([a[:N], b[:N]], axis=0)
        return carry

    lax.fori_loop(0, 36 // UA, stage_a, 0)

    def stage_b(step, carry):
        for u in range(UB):
            b = (step * UB + u) * 2
            planes = [pad_rows(work[pl.ds(b + i, N, stride=N), :]) for i in range(2)]
            planes = left_dot(tl[...], planes)
            for i in range(2):
                total = sq_rows[...] + sq_pair[pl.ds(b + i, 1), :]
                positive = total > 0
                kern = jnp.where(positive, (-0.25 * math.pi) / jnp.where(positive, total, 1.0), 0.0)
                planes[i] = planes[i] * kern
            planes = left_dot(til[...], planes)
            for i in range(2):
                work[pl.ds(b + i, N, stride=N), :] = planes[i][:N]
        return carry

    lax.fori_loop(0, 36 // UB, stage_b, 0)

    def stage_c(step, carry):
        for u in range(UC):
            base = pl.multiple_of((step * UC + u) * 2 * N, 8)
            rows = pl.ds(base, 2 * N)
            v = work[rows, :]
            a, b = left_dot(til[...], [pad_rows(v[:N]), pad_rows(v[N:])])
            z = right_dot(jnp.concatenate([a[:N], b[:N]], axis=0), tir[...])
            own[rows, :] = z * lent[rows, :]
        return carry

    lax.fori_loop(0, 36 // UC, stage_c, 0)


def from_plane(ref, dst, slab):
    for y in range(N):
        dst[pl.ds(slab * 2592 + y, 36, stride=N), :N] = ref[:, N * y : N * y + N]


def spans():
    for j in range(81):
        first, at = divmod(N * j, 1458)
        fit = min(N, 1458 - at)
        yield j, first, at, fit


def from_blocks(ref, dst, slab):
    for j, first, at, fit in spans():
        rows = pl.ds(slab * 2592 + j, 32, stride=81)
        v = ref[first, :, at : at + fit]
        if fit < N:
            v = jnp.concatenate([v, ref[first + 1, :, : N - fit]], axis=1)
        dst[rows, :N] = v


def to_blocks(src, ref, slab):
    for h in range(4):
        for j, first, at, fit in spans():
            v = src[pl.ds(slab * 2592 + 81 * h + j, 8, stride=324), :]
            ref[4 * first + h, :, at : at + fit] = v[:, :fit]
            if fit < N:
                ref[4 * first + 4 + h, :, : N - fit] = v[:, fit:N]


def fft_kernel(U, whole, lent_in, tl, til, tr, tir, sq_rows, sq_pair, out, own, lent, work):
    for s in range(2):
        from_plane(whole.at[s], own, s)
        from_blocks(lent_in.at[s], lent, s)
    convolve(own, lent, work, tl, til, tr, tir, sq_rows, sq_pair, *U)
    for s in range(2):
        to_blocks(own, out.at[s], s)


def fft_call(whole, lent, U=(9, 9, 9)):
    vm = pl.BlockSpec(memory_space=pltpu.VMEM)
    return pl.pallas_call(
        functools.partial(fft_kernel, U),
        out_shape=jax.ShapeDtypeStruct((2, 16, 8, 1458), F32),
        in_specs=[vm] * 8,
        out_specs=vm,
        scratch_shapes=[pltpu.VMEM((5184, 128), F32) for _ in range(3)],
        compiler_params=pltpu.CompilerParams(vmem_limit_bytes=48 << 20),
    )(whole, lent, *tables())


MESH = pl.DeviceIdType.MESH
BANDS = 128
CELLS = 1458
CUT = 768


def send(src, dst, send_sem, recv_sem, device):
    return pltpu.make_async_remote_copy(
        src_ref=src, dst_ref=dst, send_sem=send_sem, recv_sem=recv_sem, device_id=device, device_id_type=MESH
    )


def greet(barrier, device):
    pl.semaphore_signal(barrier, inc=1, device_id=device, device_id_type=MESH)


class Place:
    def __init__(self):
        self.band, self.grid = lax.axis_index("band"), lax.axis_index("grid")
        self.p, self.q = lax.div(self.band, 16), lax.rem(self.band, 16)
        self.z, self.core = lax.div(self.q, 2), lax.rem(self.q, 2)
        self.xh, self.y = lax.div(self.p, 4), lax.rem(self.p, 4)
        self.twin = {"band": self.band + 1 - 2 * self.core}


def device(p, q, grid):
    return {"band": p * 16 + q, "grid": grid}


def meet(me):
    barrier = pltpu.get_barrier_semaphore()

    def near(k, carry):
        w = lax.rem(me.q * 2 + me.grid + k, 32)
        greet(barrier, device(me.p, lax.div(w, 2), lax.rem(w, 2)))
        return carry

    lax.fori_loop(1, 32, near, 0)

    def far(k, carry):
        p = lax.rem(me.p + k, 8)
        for n in range(4):
            greet(barrier, device(p, me.z * 2 + n // 2, n % 2))
        return carry

    lax.fori_loop(1, 8, far, 0)
    return barrier


MET = 31 + 28


def lane_parts():
    return pl.ds(0, CUT), pl.ds(CUT, CELLS - CUT)


def exchange(me, blocks, via_a, via_b, cols, slot, grid_to, sems):
    s1, r1, s2, r2, s3, r3, s4, r4, local = sems
    low, high = lane_parts()
    stays = jnp.logical_and(slot == me.q, grid_to == me.grid)
    moves = jnp.logical_not(stays)

    def seat(q):
        return lax.rem(q, 4) * 4 + lax.div(q, 4)

    def a1(k, p_to, p_from):
        return send(blocks.at[:, p_to, low], via_a.at[p_from], s1.at[k], r1.at[k], device(p_to, slot, grid_to))

    def b1(k, q_to, q_from):
        return send(blocks.at[seat(q_to), :, high], via_b.at[q_from], s2.at[k], r2.at[q_from], device(me.p, q_to, grid_to))

    def a2(k, q_to, q_from):
        return send(via_a.at[:, seat(q_to), :], cols.at[:, q_from, low], s3.at[k], r3.at[k], device(me.p, q_to, me.grid))

    def b2(k, p_to, p_from):
        return send(via_b.at[:, p_to, :], cols.at[p_from, :, high], s4.at[k], r4.at[k], device(p_to, me.q, me.grid))

    keep_a1 = pltpu.make_async_copy(blocks.at[:, me.p, low], via_a.at[me.p], local.at[0])
    keep_b1 = pltpu.make_async_copy(blocks.at[seat(me.q), :, high], via_b.at[me.q], local.at[1])
    keep_a2 = pltpu.make_async_copy(via_a.at[:, seat(me.q), :], cols.at[:, me.q, low], local.at[2])
    keep_b2 = pltpu.make_async_copy(via_b.at[:, me.p, :], cols.at[me.p, :, high], local.at[3])

    for k in range(1, 8):
        a1(k, lax.rem(me.p + k, 8), me.p).start()
    for k in range(1, 16):
        b1(k, lax.rem(me.q + k, 16), slot).start()

    @pl.when(stays)
    def _():
        keep_a1.start()
        keep_b1.start()

    @pl.when(moves)
    def _():
        a1(0, me.p, me.p).start()
        b1(0, me.q, slot).start()

    def middle_a():
        for k in range(1, 8):
            a1(k, me.p, lax.rem(me.p + 8 - k, 8)).wait_recv()

        @pl.when(stays)
        def _():
            keep_a1.wait()

        @pl.when(moves)
        def _():
            a1(0, me.p, me.p).wait_recv()

        for k in range(1, 16):
            a2(k, lax.rem(me.q + k, 16), me.q).start()
        keep_a2.start()

    def middle_b():
        for k in range(1, 16):
            b1(k, me.q, lax.rem(me.q + k, 16)).wait_recv()

        @pl.when(stays)
        def _():
            keep_b1.wait()

        @pl.when(moves)
        def _():
            b1(0, me.q, me.q).wait_recv()

        for k in range(1, 8):
            b2(k, lax.rem(me.p + k, 8), me.p).start()
        keep_b2.start()

    def finish():
        for k in range(1, 16):
            a2(k, me.q, lax.rem(me.q + 16 - k, 16)).wait_recv()
        for k in range(1, 8):
            b2(k, me.p, lax.rem(me.p + 8 - k, 8)).wait_recv()
        keep_a2.wait()
        keep_b2.wait()

    def drain():
        for k in range(1, 8):
            a1(k, lax.rem(me.p + k, 8), me.p).wait_send()
            b2(k, lax.rem(me.p + k, 8), me.p).wait_send()
        for k in range(1, 16):
            b1(k, lax.rem(me.q + k, 16), slot).wait_send()
            a2(k, lax.rem(me.q + k, 16), me.q).wait_send()

        @pl.when(moves)
        def _():
            a1(0, me.p, me.p).wait_send()
            b1(0, me.q, slot).wait_send()

    return middle_a, middle_b, finish, drain


def exchange_scratch():
    dma = pltpu.SemaphoreType.DMA
    return [
        pltpu.VMEM((8, 16, CUT), F32), pltpu.VMEM((16, 8, CELLS - CUT), F32),
        dma((8,)), dma((8,)), dma((16,)), dma((16,)), dma((16,)), dma((16,)), dma((8,)), dma((8,)), dma((4,)),
    ]


def gather_lent(me, picked, lent, send_sem, recv_sem, local):
    zlo, zhi = lax.rem(me.z, 2), lax.div(me.z, 2)

    def cell(q):
        z = lax.div(q, 2)
        return lent.at[me.grid, lax.rem(z, 2), lax.rem(q, 2), me.xh, pl.ds(4 * me.y + lax.div(z, 2), 1), :]

    def over_q(k, q_to, q_from):
        return send(
            picked.at[pl.ds(lax.rem(q_to, 2), 1), :], cell(q_from), send_sem.at[k], recv_sem.at[k],
            device(me.p, q_to, me.grid),
        )

    keep = pltpu.make_async_copy(picked.at[pl.ds(me.core, 1), :], cell(me.q), local)
    for k in range(1, 16):
        over_q(k, lax.rem(me.q + k, 16), me.q).start()
    keep.start()
    for k in range(1, 16):
        over_q(k, me.q, lax.rem(me.q + 16 - k, 16)).wait_recv()
    keep.wait()

    def piece(half, grid, xh, y):
        return lent.at[grid, :, half, xh, pl.ds(4 * y, 4), :]

    started = []

    def x_peer(n):
        return lax.rem(me.xh + n // 2, 2), lax.rem(me.grid + n, 2)

    def along_x(slot, half, y, n):
        xh, grid = x_peer(n)
        part = piece(half, me.grid, me.xh, y)
        return send(part, part, send_sem.at[slot + n], recv_sem.at[slot + n], device(4 * xh + me.y, me.q, grid))

    def from_x(slot, half, y, n):
        xh, grid = x_peer(n)
        part = piece(half, grid, xh, y)
        return send(part, part, send_sem.at[slot + n], recv_sem.at[slot + n], device(4 * xh + me.y, me.q, grid))

    def along_y(slot, half, xh, grid, n):
        part = piece(half, grid, xh, me.y)
        return send(part, part, send_sem.at[slot + n], recv_sem.at[slot + n], device(4 * me.xh + lax.rem(me.y + n, 4), me.q, me.grid))

    def from_y(slot, half, xh, grid, n):
        part = piece(half, grid, xh, lax.rem(me.y + 4 - n, 4))
        return send(part, part, send_sem.at[slot + n], recv_sem.at[slot + n], device(4 * me.xh + lax.rem(me.y + n, 4), me.q, me.grid))

    def go(copy):
        copy.start()
        started.append(copy)

    for n in range(1, 4):
        go(along_x(16, 0, me.y, n))
        go(along_y(20, 1, me.xh, me.grid, n))
    for n in range(1, 4):
        go(along_y(24, 0, me.xh, me.grid, n))
        go(along_x(40, 1, me.y, n))
    for m in range(1, 4):
        from_x(16, 0, me.y, m).wait_recv()
        xh, grid = x_peer(m)
        for n in range(1, 4):
            go(along_y(24 + 4 * m, 0, xh, grid, n))
        from_y(20, 1, me.xh, me.grid, m).wait_recv()
        for n in range(1, 4):
            go(along_x(40 + 4 * m, 1, lax.rem(me.y + 4 - m, 4), n))
    for m in range(4):
        xh, grid = x_peer(m)
        for n in range(1, 4):
            from_y(24 + 4 * m, 0, xh, grid, n).wait_recv()
            from_x(40 + 4 * m, 1, lax.rem(me.y + 4 - m, 4), n).wait_recv()

    def drain():
        for k in range(1, 16):
            over_q(k, lax.rem(me.q + k, 16), me.q).wait_send()
        for c in started:
            c.wait_send()

    return drain


def lend_kernel(
    owners, orb, cols, whole, lent, rows, blocks, picked, own_sem, w_send, w_recv, g_send, g_recv,
    via_a, via_b, *sems,
):
    me = Place()
    partner = {"grid": 1 - me.grid}
    barrier = meet(me)
    from_plane(orb, rows, 0)
    to_blocks(rows, blocks, 0)
    pl.semaphore_wait(barrier, MET)
    same = me.core == me.grid
    differ = jnp.logical_not(same)
    middle_a, middle_b, finish, drain = exchange(me, blocks, via_a, via_b, cols, me.q, me.grid, sems)
    keep = pltpu.make_async_copy(orb, whole.at[me.grid], own_sem.at[0])
    to_twin = send(orb, whole.at[me.grid], w_send.at[0], w_recv.at[0], me.twin)
    to_partner = send(orb, whole.at[me.grid], w_send.at[0], w_recv.at[1], partner)
    from_partner = send(orb, whole.at[1 - me.grid], w_send.at[0], w_recv.at[1], partner)
    forward = send(whole.at[1 - me.grid], whole.at[1 - me.grid], w_send.at[1], w_recv.at[1], me.twin)

    @pl.when(same)
    def _():
        keep.start()
        to_twin.start()

    @pl.when(differ)
    def _():
        to_partner.start()

    middle_a()
    middle_b()
    finish()
    for r in range(2):
        owner = owners[r]
        picked[r : r + 1, :] = cols[pl.ds(lax.div(owner, 16), 1), pl.ds(lax.rem(owner, 16), 1), :].reshape(1, CELLS)

    @pl.when(same)
    def _():
        from_partner.wait_recv()
        forward.start()

    drain_gather = gather_lent(me, picked, lent, g_send, g_recv, own_sem.at[1])

    @pl.when(same)
    def _():
        keep.wait()
        to_twin.wait_send()
        forward.wait_send()

    @pl.when(differ)
    def _():
        to_twin.wait_recv()
        forward.wait_recv()
        to_partner.wait_send()

    drain_gather()
    drain()


def lend_call(owners, orb):
    vm = pl.BlockSpec(memory_space=pltpu.VMEM)
    dma = pltpu.SemaphoreType.DMA
    return pl.pallas_call(
        lend_kernel,
        out_shape=(
            jax.ShapeDtypeStruct((8, 16, CELLS), F32),
            jax.ShapeDtypeStruct((2, 36, 5184), F32),
            jax.ShapeDtypeStruct((2, 2, 2, 2, 16, CELLS), F32),
        ),
        in_specs=[pl.BlockSpec(memory_space=pltpu.SMEM), vm],
        out_specs=(vm, vm, vm),
        scratch_shapes=[
            pltpu.VMEM((2592, 128), F32), pltpu.VMEM((16, 8, CELLS), F32), pltpu.VMEM((2, CELLS), F32),
            dma((2,)), dma((2,)), dma((2,)), dma((56,)), dma((56,)),
        ] + exchange_scratch(),
        compiler_params=pltpu.CompilerParams(collective_id=0, has_side_effects=True, vmem_limit_bytes=40 << 20),
    )(owners, orb)


def add_up(me, product, matrix, first, second, m_send, m_recv):
    p, q, grid = me.p, me.q, me.grid

    def block(c):
        return pl.ds(pl.multiple_of(8 * c, 8), 8)

    def scatter(k, to, slot):
        return send(product.at[block(to), :], first.at[slot], m_send.at[k], m_recv.at[k], device(p, to, grid))

    for k in range(1, 16):
        scatter(k, lax.rem(q + k, 16), q).start()
    first[q] = product[block(q), :]
    for k in range(1, 16):
        scatter(k, q, lax.rem(q + 16 - k, 16)).wait_recv()
    total = first[0]
    for k in range(1, 16):
        total = total + first[k]
    where = 2 * p + grid
    second[where] = total

    def share(k, slot, p_to, g_to):
        return send(second.at[slot], second.at[slot], m_send.at[15 + k], m_recv.at[15 + k], device(p_to, q, g_to))

    for k in range(1, 16):
        share(k, where, lax.rem(p + k // 2, 8), lax.rem(grid + k, 2)).start()
    for k in range(1, 16):
        p_, g_ = lax.rem(p + 8 - k // 2, 8), lax.rem(grid + k, 2)
        share(k, 2 * p_ + g_, p_, g_).wait_recv()
    total = second[0]
    for k in range(1, 16):
        total = total + second[k]
    matrix[block(q), :] = total

    def spread(k, to, slot):
        return send(
            matrix.at[block(slot), :], matrix.at[block(slot), :], m_send.at[30 + k], m_recv.at[30 + k],
            device(p, to, grid),
        )

    for k in range(1, 16):
        spread(k, lax.rem(q + k, 16), q).start()
    for k in range(1, 16):
        spread(k, q, lax.rem(q + 16 - k, 16)).wait_recv()

    for k in range(1, 16):
        scatter(k, lax.rem(q + k, 16), q).wait_send()
        share(k, where, lax.rem(p + k // 2, 8), lax.rem(grid + k, 2)).wait_send()
        spread(k, lax.rem(q + k, 16), q).wait_send()


def matrix_kernel(
    part, cols, field, matrix, summed, arrived, product, first, second, t_send, t_recv, m_send, m_recv,
    via_a, via_b, *sems,
):
    me = Place()
    barrier = meet(me)
    pl.semaphore_wait(barrier, MET)

    def give(n):
        piece = pl.ds(4 * n, 4)
        return send(part.at[1 - me.core, piece], arrived.at[piece], t_send.at[n], t_recv.at[n], me.twin)

    for n in range(4):
        give(n).start()
    for n in range(4):
        give(n).wait_recv()
        piece = pl.ds(4 * n, 4)
        summed[piece] = part[me.core, piece] + arrived[piece]
    middle_a, middle_b, finish, drain = exchange(
        me, summed, via_a, via_b, field, 2 * me.z + me.grid, me.core, sems
    )
    middle_a()
    middle_b()
    finish()
    oh, ol = halves(cols[...].reshape(BANDS, CELLS))
    fh, fl = halves(field[...].reshape(BANDS, CELLS))
    dot = lambda a, b: lax.dot_general(a, b, (((1,), (1,)), ((), ())), preferred_element_type=F32)
    product[...] = ((dot(oh, fl) + dot(ol, fh)) + dot(oh, fh)) * (1.0 / 373248.0)
    add_up(me, product, matrix, first, second, m_send, m_recv)
    for n in range(4):
        give(n).wait_send()
    drain()


def matrix_call(part, cols):
    vm = pl.BlockSpec(memory_space=pltpu.VMEM)
    dma = pltpu.SemaphoreType.DMA
    return pl.pallas_call(
        matrix_kernel,
        out_shape=(
            jax.ShapeDtypeStruct((8, 16, CELLS), F32),
            jax.ShapeDtypeStruct((BANDS, BANDS), F32),
        ),
        in_specs=[vm, vm],
        out_specs=(vm, vm),
        scratch_shapes=[
            pltpu.VMEM((16, 8, CELLS), F32), pltpu.VMEM((16, 8, CELLS), F32), pltpu.VMEM((BANDS, BANDS), F32),
            pltpu.VMEM((16, 8, BANDS), F32), pltpu.VMEM((16, 8, BANDS), F32),
            dma((4,)), dma((4,)), dma((46,)), dma((46,)),
        ] + exchange_scratch(),
        compiler_params=pltpu.CompilerParams(collective_id=1, has_side_effects=True, vmem_limit_bytes=40 << 20),
    )(part, cols)


def shards(orbitals, owners):
    cols, whole, lent = lend_call(owners, orbitals[0])
    part = fft_call(whole, lent.reshape(2, 4, 32, CELLS))
    field, matrix = matrix_call(part, cols)
    return (field.reshape(1, BANDS, CELLS), matrix)


def solution(mesh):
    in_specs = (P("band", "grid", None), P())
    out_specs = (P("grid", None, "band"), P())
    return jax.shard_map(shards, mesh=mesh, in_specs=in_specs, out_specs=out_specs, check_vma=False)
```

time: 146 us -> 118 us (0.81)
  Pallas kernels: 141 us -> 113 us
    pallas_call x2, Pallas kernels: 127 us -> 99 us  [the longest x1 52.7 us: lend_call(): pl.pallas_call(lend_kernel, out_shape=(jax.ShapeDtypeStruct((8, 16, CELLS...]
where the time goes in v3:
time: 118 us
  Pallas kernels  113 us (96%)
  local copies, waits for them, and re-layouts  3.71 us (3%)
    pallas_call x1, Pallas kernels, lend_call(): pl.pallas_call(lend_kernel, out_shape=(jax.ShapeDtypeStruct((8, 16, CELLS...  52.7 us
    pallas_call x1, Pallas kernels, matrix_call(): pl.pallas_call(matrix_kernel, out_shape=(jax.ShapeDtypeStruct((8, 16, CEL...  46.3 us
    pallas_call x1, Pallas kernels, fft_call(): pl.pallas_call(functools.partial(fft_kernel, U), out_shape=jax.ShapeDtype...  14.3 us
    unnamed x17, local copies, waits for them, and re-layouts  3.71 us

profile of v3, /device:TPU:1, one launch (start us, length us, event | category | flops | bytes accessed | tf_op | source)
XLA Modules:
  0.0 117.8 jit_solution(1347181267437260159)
XLA Ops:
  0.6 0.0 copy-start
  0.6 0.0 copy-start.1
  0.7 0.0 copy-start.2
  0.7 0.0 copy-start.3
  0.7 0.0 copy-start.5
  0.7 0.0 copy-start.4
  0.7 0.0 copy-start.6
  0.7 1.3 %copy.17 = f32[1,36,5184]{2,1,0:T(8,128)S(1)} copy(f32[1,36,5184]{2,0,1:T(1,128)} %param.12) | data formatting | bytes 1492992
  2.0 0.0 copy-done.6
  2.0 52.7 %shard_map.131 = (f32[8,16,1458]{2,1,0:T(8,128)S(1)}, f32[2,36,5184]{2,1,0:T(8,128)S(1)}, f32[2,2,2,2,16,1458]{5,4,3,2,1,0:T(8,128)S(1)}) custom-call(s32[128]{0:T(128)S(1)} %copy-done.6, f32[36,5184]{1,0:T(8,128)S(1)} %bitcast.5), custom_call_target="tpu_custom_call" | custom-call | tf_op jit(solution)/shard_map/pallas_call | solution.py:471
  54.8 0.0 copy-done
  54.8 0.0 copy-done.1
  54.8 0.0 copy-done.2
  54.8 0.0 copy-done.3
  54.8 0.0 copy-done.5
  54.8 0.0 copy-done.4
  54.8 14.3 %shard_map.132.part = f32[2,16,8,1458]{3,2,1,0:T(8,128)S(1)} custom-call(f32[2,36,5184]{2,1,0:T(8,128)S(1)} %get-tuple-element.7.whole, f32[2,4,32,1458]{3,2,1,0:T(8,128)S(1)} %bitcast.6, bf16[80,240]{1,0:T(8,128)(2,1)S(1)} %copy-done.3, bf16[80,240]{1,0:T(8,128)(2,1)S(1)} %copy-done.2, bf16[256,256]{1,0:T(8,128)(2,1)S(1)} %copy-done.1, ...), custom_call_target="tpu_custom_call" | custom-call | tf_op jit(solution)/shard_map/pallas_call | solution.py:159
  69.2 46.3 %shard_map.133 = (f32[8,16,1458]{2,1,0:T(8,128)S(1)}, f32[128,128]{1,0:T(8,128)S(1)}) custom-call(f32[2,16,8,1458]{3,2,1,0:T(8,128)S(1)} %shard_map.132.part, f32[8,16,1458]{2,1,0:T(8,128)S(1)} %get-tuple-element.9.cols), custom_call_target="tpu_custom_call" | custom-call | tf_op jit(solution)/shard_map/pallas_call | solution.py:575
  115.4 1.7 %copy.14 = f32[1,128,1458]{1,0,2:T(1,128)} copy(f32[1,128,1458]{2,1,0:T(8,128)S(1)} %bitcast.7) | data formatting | bytes 1492992
  117.1 0.6 copy.19
Async XLA Ops:
  0.6 54.2 %copy-start = (bf16[256,256]{1,0:T(8,128)(2,1)S(1)}, bf16[256,256]{1,0:T(8,128)(2,1)}, u32[]{:S(2)}) copy-start(bf16[256,256]{1,0:T(8,128)(2,1)} %constant.60.tir) | copy-start | bytes 393220
  0.6 54.2 %copy-start.1 = (bf16[256,256]{1,0:T(8,128)(2,1)S(1)}, bf16[256,256]{1,0:T(8,128)(2,1)}, u32[]{:S(2)}) copy-start(bf16[256,256]{1,0:T(8,128)(2,1)} %constant.55.tr) | copy-start | bytes 393220
  0.7 54.1 %copy-start.2 = (bf16[80,240]{1,0:T(8,128)(2,1)S(1)}, bf16[80,240]{1,0:T(8,128)(2,1)}, u32[]{:S(2)}) copy-start(bf16[80,240]{1,0:T(8,128)(2,1)} %constant.50.til) | copy-start | bytes 115204
  0.7 54.1 %copy-start.3 = (bf16[80,240]{1,0:T(8,128)(2,1)S(1)}, bf16[80,240]{1,0:T(8,128)(2,1)}, u32[]{:S(2)}) copy-start(bf16[80,240]{1,0:T(8,128)(2,1)} %constant.43.tl) | copy-start | bytes 115204
  0.7 54.1 %copy-start.5 = (f32[72,128]{1,0:T(8,128)S(1)}, f32[72,128]{1,0:T(8,128)}, u32[]{:S(2)}) copy-start(f32[72,128]{1,0:T(8,128)} %constant.15.clone.sq_pair) | copy-start | bytes 110596
  0.7 54.1 %copy-start.4 = (f32[80,128]{1,0:T(8,128)S(1)}, f32[80,128]{1,0:T(8,128)}, u32[]{:S(2)}) copy-start(f32[80,128]{1,0:T(8,128)} %constant.14.clone.sq_rows) | copy-start | bytes 122884
  0.7 1.3 %copy-start.6 = (s32[128]{0:T(128)S(1)}, s32[128]{0:T(128)}, u32[]{:S(2)}) copy-start(s32[128]{0:T(128)} %owners.1) | copy-start | bytes 1540

commit v4 on v3

--- a/solution.py
+++ b/solution.py
@@ -70,7 +70,7 @@
     return jnp.concatenate([v, jnp.zeros((PAD - N, 128), F32)], axis=0)
 
 
-def convolve(own, lent, work, tl, til, tr, tir, sq_rows, sq_pair, UA, UB, UC):
+def spectra(own, lent, work, tl, til, tr, sq_rows, sq_pair, UA, UB):
     lane = lax.broadcasted_iota(jnp.int32, (1, 128), 1) < N
 
     def stage_a(step, carry):
@@ -102,9 +102,11 @@
 
     lax.fori_loop(0, 36 // UB, stage_b, 0)
 
+
+def potentials(own, lent, work, til, tir, slab, UC):
     def stage_c(step, carry):
         for u in range(UC):
-            base = pl.multiple_of((step * UC + u) * 2 * N, 8)
+            base = pl.multiple_of(slab * 2592 + (step * UC + u) * 2 * N, 8)
             rows = pl.ds(base, 2 * N)
             v = work[rows, :]
             a, b = left_dot(til[...], [pad_rows(v[:N]), pad_rows(v[N:])])
@@ -112,7 +114,7 @@
             own[rows, :] = z * lent[rows, :]
         return carry
 
-    lax.fori_loop(0, 36 // UC, stage_c, 0)
+    lax.fori_loop(0, 18 // UC, stage_c, 0)
 
 
 def from_plane(ref, dst, slab):
@@ -130,9 +132,9 @@
 def from_blocks(ref, dst, slab):
     for j, first, at, fit in spans():
         rows = pl.ds(slab * 2592 + j, 32, stride=81)
-        v = ref[first, :, at : at + fit]
+        v = ref[first // 2, first % 2, :, at : at + fit]
         if fit < N:
-            v = jnp.concatenate([v, ref[first + 1, :, : N - fit]], axis=1)
+            v = jnp.concatenate([v, ref[(first + 1) // 2, (first + 1) % 2, :, : N - fit]], axis=1)
         dst[rows, :N] = v
 
 
@@ -145,27 +147,6 @@
                 ref[4 * first + 4 + h, :, : N - fit] = v[:, fit:N]
 
 
-def fft_kernel(U, whole, lent_in, tl, til, tr, tir, sq_rows, sq_pair, out, own, lent, work):
-    for s in range(2):
-        from_plane(whole.at[s], own, s)
-        from_blocks(lent_in.at[s], lent, s)
-    convolve(own, lent, work, tl, til, tr, tir, sq_rows, sq_pair, *U)
-    for s in range(2):
-        to_blocks(own, out.at[s], s)
-
-
-def fft_call(whole, lent, U=(9, 9, 9)):
-    vm = pl.BlockSpec(memory_space=pltpu.VMEM)
-    return pl.pallas_call(
-        functools.partial(fft_kernel, U),
-        out_shape=jax.ShapeDtypeStruct((2, 16, 8, 1458), F32),
-        in_specs=[vm] * 8,
-        out_specs=vm,
-        scratch_shapes=[pltpu.VMEM((5184, 128), F32) for _ in range(3)],
-        compiler_params=pltpu.CompilerParams(vmem_limit_bytes=48 << 20),
-    )(whole, lent, *tables())
-
-
 MESH = pl.DeviceIdType.MESH
 BANDS = 128
 CELLS = 1458
@@ -327,12 +308,12 @@
     ]
 
 
-def gather_lent(me, picked, lent, send_sem, recv_sem, local):
+def gather_lent(me, picked, lent, send_sem, recv_sem, local, meanwhile):
     zlo, zhi = lax.rem(me.z, 2), lax.div(me.z, 2)
 
     def cell(q):
         z = lax.div(q, 2)
-        return lent.at[me.grid, lax.rem(z, 2), lax.rem(q, 2), me.xh, pl.ds(4 * me.y + lax.div(z, 2), 1), :]
+        return lent.at[me.grid, lax.rem(z, 2), lax.rem(q, 2), pl.ds(4 * me.p + lax.div(z, 2), 1), :]
 
     def over_q(k, q_to, q_from):
         return send(
@@ -349,7 +330,7 @@
     keep.wait()
 
     def piece(half, grid, xh, y):
-        return lent.at[grid, :, half, xh, pl.ds(4 * y, 4), :]
+        return lent.at[grid, :, half, pl.ds(16 * xh + 4 * y, 4), :]
 
     started = []
 
@@ -392,6 +373,7 @@
         from_y(20, 1, me.xh, me.grid, m).wait_recv()
         for n in range(1, 4):
             go(along_x(40 + 4 * m, 1, lax.rem(me.y + 4 - m, 4), n))
+    meanwhile()
     for m in range(4):
         xh, grid = x_peer(m)
         for n in range(1, 4):
@@ -407,19 +389,73 @@
     return drain
 
 
-def lend_kernel(
-    owners, orb, cols, whole, lent, rows, blocks, picked, own_sem, w_send, w_recv, g_send, g_recv,
-    via_a, via_b, *sems,
+def add_up(me, product, matrix, first, second, m_send, m_recv):
+    p, q, grid = me.p, me.q, me.grid
+
+    def block(c):
+        return pl.ds(pl.multiple_of(8 * c, 8), 8)
+
+    def scatter(k, to, slot):
+        return send(product.at[block(to), :], first.at[slot], m_send.at[k], m_recv.at[k], device(p, to, grid))
+
+    for k in range(1, 16):
+        scatter(k, lax.rem(q + k, 16), q).start()
+    first[q] = product[block(q), :]
+    for k in range(1, 16):
+        scatter(k, q, lax.rem(q + 16 - k, 16)).wait_recv()
+    total = first[0]
+    for k in range(1, 16):
+        total = total + first[k]
+    where = 2 * p + grid
+    second[where] = total
+
+    def share(k, slot, p_to, g_to):
+        return send(second.at[slot], second.at[slot], m_send.at[15 + k], m_recv.at[15 + k], device(p_to, q, g_to))
+
+    for k in range(1, 16):
+        share(k, where, lax.rem(p + k // 2, 8), lax.rem(grid + k, 2)).start()
+    for k in range(1, 16):
+        p_, g_ = lax.rem(p + 8 - k // 2, 8), lax.rem(grid + k, 2)
+        share(k, 2 * p_ + g_, p_, g_).wait_recv()
+    total = second[0]
+    for k in range(1, 16):
+        total = total + second[k]
+    matrix[block(q), :] = total
+
+    def spread(k, to, slot):
+        return send(
+            matrix.at[block(slot), :], matrix.at[block(slot), :], m_send.at[30 + k], m_recv.at[30 + k],
+            device(p, to, grid),
+        )
+
+    for k in range(1, 16):
+        spread(k, lax.rem(q + k, 16), q).start()
+    for k in range(1, 16):
+        spread(k, q, lax.rem(q + 16 - k, 16)).wait_recv()
+
+    for k in range(1, 16):
+        scatter(k, lax.rem(q + k, 16), q).wait_send()
+        share(k, where, lax.rem(p + k // 2, 8), lax.rem(grid + k, 2)).wait_send()
+        spread(k, lax.rem(q + k, 16), q).wait_send()
+
+
+def fock_kernel(
+    owners, orb, tl, til, tr, tir, sq_rows, sq_pair, field, matrix,
+    cols, whole, lent, blocks, picked, own_rows, lent_rows, work,
+    given, kept, arrived, product, first, second,
+    own_sem, w_send, w_recv, g_send, g_recv, t_send, t_recv, m_send, m_recv, *rest,
 ):
+    near, far = rest[: len(rest) // 2], rest[len(rest) // 2 :]
     me = Place()
     partner = {"grid": 1 - me.grid}
     barrier = meet(me)
-    from_plane(orb, rows, 0)
-    to_blocks(rows, blocks, 0)
+    from_plane(orb, work, 0)
+    to_blocks(work, blocks, 0)
     pl.semaphore_wait(barrier, MET)
+
     same = me.core == me.grid
     differ = jnp.logical_not(same)
-    middle_a, middle_b, finish, drain = exchange(me, blocks, via_a, via_b, cols, me.q, me.grid, sems)
+    middle_a, middle_b, finish, drain_near = exchange(me, blocks, near[0], near[1], cols, me.q, me.grid, near[2:])
     keep = pltpu.make_async_copy(orb, whole.at[me.grid], own_sem.at[0])
     to_twin = send(orb, whole.at[me.grid], w_send.at[0], w_recv.at[0], me.twin)
     to_partner = send(orb, whole.at[me.grid], w_send.at[0], w_recv.at[1], partner)
@@ -447,114 +483,35 @@
         from_partner.wait_recv()
         forward.start()
 
-    drain_gather = gather_lent(me, picked, lent, g_send, g_recv, own_sem.at[1])
-
-    @pl.when(same)
-    def _():
-        keep.wait()
-        to_twin.wait_send()
-        forward.wait_send()
-
-    @pl.when(differ)
-    def _():
-        to_twin.wait_recv()
-        forward.wait_recv()
-        to_partner.wait_send()
-
-    drain_gather()
-    drain()
-
-
-def lend_call(owners, orb):
-    vm = pl.BlockSpec(memory_space=pltpu.VMEM)
-    dma = pltpu.SemaphoreType.DMA
-    return pl.pallas_call(
-        lend_kernel,
-        out_shape=(
-            jax.ShapeDtypeStruct((8, 16, CELLS), F32),
-            jax.ShapeDtypeStruct((2, 36, 5184), F32),
-            jax.ShapeDtypeStruct((2, 2, 2, 2, 16, CELLS), F32),
-        ),
-        in_specs=[pl.BlockSpec(memory_space=pltpu.SMEM), vm],
-        out_specs=(vm, vm, vm),
-        scratch_shapes=[
-            pltpu.VMEM((2592, 128), F32), pltpu.VMEM((16, 8, CELLS), F32), pltpu.VMEM((2, CELLS), F32),
-            dma((2,)), dma((2,)), dma((2,)), dma((56,)), dma((56,)),
-        ] + exchange_scratch(),
-        compiler_params=pltpu.CompilerParams(collective_id=0, has_side_effects=True, vmem_limit_bytes=40 << 20),
-    )(owners, orb)
-
-
-def add_up(me, product, matrix, first, second, m_send, m_recv):
-    p, q, grid = me.p, me.q, me.grid
-
-    def block(c):
-        return pl.ds(pl.multiple_of(8 * c, 8), 8)
-
-    def scatter(k, to, slot):
-        return send(product.at[block(to), :], first.at[slot], m_send.at[k], m_recv.at[k], device(p, to, grid))
-
-    for k in range(1, 16):
-        scatter(k, lax.rem(q + k, 16), q).start()
-    first[q] = product[block(q), :]
-    for k in range(1, 16):
-        scatter(k, q, lax.rem(q + 16 - k, 16)).wait_recv()
-    total = first[0]
-    for k in range(1, 16):
-        total = total + first[k]
-    where = 2 * p + grid
-    second[where] = total
-
-    def share(k, slot, p_to, g_to):
-        return send(second.at[slot], second.at[slot], m_send.at[15 + k], m_recv.at[15 + k], device(p_to, q, g_to))
-
-    for k in range(1, 16):
-        share(k, where, lax.rem(p + k // 2, 8), lax.rem(grid + k, 2)).start()
-    for k in range(1, 16):
-        p_, g_ = lax.rem(p + 8 - k // 2, 8), lax.rem(grid + k, 2)
-        share(k, 2 * p_ + g_, p_, g_).wait_recv()
-    total = second[0]
-    for k in range(1, 16):
-        total = total + second[k]
-    matrix[block(q), :] = total
-
-    def spread(k, to, slot):
-        return send(
-            matrix.at[block(slot), :], matrix.at[block(slot), :], m_send.at[30 + k], m_recv.at[30 + k],
-            device(p, to, grid),
-        )
-
-    for k in range(1, 16):
-        spread(k, lax.rem(q + k, 16), q).start()
-    for k in range(1, 16):
-        spread(k, q, lax.rem(q + 16 - k, 16)).wait_recv()
-
-    for k in range(1, 16):
-        scatter(k, lax.rem(q + k, 16), q).wait_send()
-        share(k, where, lax.rem(p + k // 2, 8), lax.rem(grid + k, 2)).wait_send()
-        spread(k, lax.rem(q + k, 16), q).wait_send()
-
-
-def matrix_kernel(
-    part, cols, field, matrix, summed, arrived, product, first, second, t_send, t_recv, m_send, m_recv,
-    via_a, via_b, *sems,
-):
-    me = Place()
-    barrier = meet(me)
-    pl.semaphore_wait(barrier, MET)
-
-    def give(n):
-        piece = pl.ds(4 * n, 4)
-        return send(part.at[1 - me.core, piece], arrived.at[piece], t_send.at[n], t_recv.at[n], me.twin)
-
-    for n in range(4):
-        give(n).start()
-    for n in range(4):
-        give(n).wait_recv()
-        piece = pl.ds(4 * n, 4)
-        summed[piece] = part[me.core, piece] + arrived[piece]
-    middle_a, middle_b, finish, drain = exchange(
-        me, summed, via_a, via_b, field, 2 * me.z + me.grid, me.core, sems
+    def meanwhile():
+        @pl.when(same)
+        def _():
+            keep.wait()
+
+        @pl.when(differ)
+        def _():
+            to_twin.wait_recv()
+            forward.wait_recv()
+
+        for s in range(2):
+            from_plane(whole.at[s], own_rows, s)
+
+    drain_gather = gather_lent(me, picked, lent, g_send, g_recv, own_sem.at[1], meanwhile)
+
+    for s in range(2):
+        from_blocks(lent.at[s], lent_rows, s)
+    spectra(own_rows, lent_rows, work, tl, til, tr, sq_rows, sq_pair, 9, 9)
+    potentials(own_rows, lent_rows, work, til, tir, 1 - me.core, 9)
+    to_blocks(own_rows, given, 1 - me.core)
+    give = send(given, arrived, t_send, t_recv, me.twin)
+    give.start()
+    potentials(own_rows, lent_rows, work, til, tir, me.core, 9)
+    to_blocks(own_rows, kept, me.core)
+    give.wait_recv()
+    kept[...] = kept[...] + arrived[...]
+
+    middle_a, middle_b, finish, drain_far = exchange(
+        me, kept, far[0], far[1], field, 2 * me.z + me.grid, me.core, far[2:]
     )
     middle_a()
     middle_b()
@@ -564,35 +521,46 @@
     dot = lambda a, b: lax.dot_general(a, b, (((1,), (1,)), ((), ())), preferred_element_type=F32)
     product[...] = ((dot(oh, fl) + dot(ol, fh)) + dot(oh, fh)) * (1.0 / 373248.0)
     add_up(me, product, matrix, first, second, m_send, m_recv)
-    for n in range(4):
-        give(n).wait_send()
-    drain()
-
-
-def matrix_call(part, cols):
+
+    @pl.when(same)
+    def _():
+        to_twin.wait_send()
+        forward.wait_send()
+
+    @pl.when(differ)
+    def _():
+        to_partner.wait_send()
+
+    give.wait_send()
+    drain_gather()
+    drain_near()
+    drain_far()
+
+
+def fock_call(owners, orb):
     vm = pl.BlockSpec(memory_space=pltpu.VMEM)
     dma = pltpu.SemaphoreType.DMA
+    v = lambda *shape: pltpu.VMEM(shape, F32)
     return pl.pallas_call(
-        matrix_kernel,
+        fock_kernel,
         out_shape=(
             jax.ShapeDtypeStruct((8, 16, CELLS), F32),
             jax.ShapeDtypeStruct((BANDS, BANDS), F32),
         ),
-        in_specs=[vm, vm],
+        in_specs=[pl.BlockSpec(memory_space=pltpu.SMEM)] + [vm] * 7,
         out_specs=(vm, vm),
         scratch_shapes=[
-            pltpu.VMEM((16, 8, CELLS), F32), pltpu.VMEM((16, 8, CELLS), F32), pltpu.VMEM((BANDS, BANDS), F32),
-            pltpu.VMEM((16, 8, BANDS), F32), pltpu.VMEM((16, 8, BANDS), F32),
-            dma((4,)), dma((4,)), dma((46,)), dma((46,)),
-        ] + exchange_scratch(),
-        compiler_params=pltpu.CompilerParams(collective_id=1, has_side_effects=True, vmem_limit_bytes=40 << 20),
-    )(part, cols)
+            v(8, 16, CELLS), v(2, 36, 5184), v(2, 2, 2, 32, CELLS), v(16, 8, CELLS), v(2, CELLS),
+            v(5184, 128), v(5184, 128), v(5184, 128),
+            v(16, 8, CELLS), v(16, 8, CELLS), v(16, 8, CELLS), v(BANDS, BANDS), v(16, 8, BANDS), v(16, 8, BANDS),
+            dma((2,)), dma((2,)), dma((2,)), dma((56,)), dma((56,)), dma, dma, dma((46,)), dma((46,)),
+        ] + exchange_scratch() + exchange_scratch(),
+        compiler_params=pltpu.CompilerParams(collective_id=0, has_side_effects=True, vmem_limit_bytes=48 << 20),
+    )(owners, orb, *tables())
 
 
 def shards(orbitals, owners):
-    cols, whole, lent = lend_call(owners, orbitals[0])
-    part = fft_call(whole, lent.reshape(2, 4, 32, CELLS))
-    field, matrix = matrix_call(part, cols)
+    field, matrix = fock_call(owners, orbitals[0])
     return (field.reshape(1, BANDS, CELLS), matrix)
 
 

time: 118 us -> 110 us (0.932)
  Pallas kernels: 113 us -> 105 us
    pallas_call x3 -> x1, Pallas kernels: 113 us -> 105 us  [fock_call(): pl.pallas_call(fock_kernel, out_shape=(jax.ShapeDtypeStruct((8, 16, CELLS...]
where the time goes in v4:
time: 110 us
  Pallas kernels  105 us (95%)
  local copies, waits for them, and re-layouts  4.26 us (4%)
    pallas_call x1, Pallas kernels, fock_call(): pl.pallas_call(fock_kernel, out_shape=(jax.ShapeDtypeStruct((8, 16, CELLS...  105 us
    unnamed x17, local copies, waits for them, and re-layouts  4.26 us

profile of v4, /device:TPU:1, one launch (start us, length us, event | category | flops | bytes accessed | tf_op | source)
XLA Modules:
  0.0 110.4 jit_solution(6183732654129843747)
XLA Ops:
  0.6 0.0 copy-start
  0.6 0.0 copy-start.1
  0.7 0.0 copy-start.2
  0.7 0.0 copy-start.3
  0.7 0.0 copy-start.4
  0.7 0.0 copy-start.5
  0.7 1.3 %copy.17 = f32[1,36,5184]{2,1,0:T(8,128)S(1)} copy(f32[1,36,5184]{2,0,1:T(1,128)} %param.12) | data formatting | bytes 1492992
  2.0 0.0 copy-start.6
  2.0 0.0 copy-done
  2.0 0.0 copy-done.1
  2.0 0.0 copy-done.2
  2.0 0.0 copy-done.3
  2.0 0.0 copy-done.4
  2.1 0.0 copy-done.5
  2.1 0.6 copy-done.6
  2.7 105.4 %shard_map.131 = (f32[8,16,1458]{2,1,0:T(8,128)S(1)}, f32[128,128]{1,0:T(8,128)S(1)}) custom-call(s32[128]{0:T(128)S(1)} %copy-done.6, f32[36,5184]{1,0:T(8,128)S(1)} %bitcast.4, bf16[80,240]{1,0:T(8,128)(2,1)S(1)} %copy-done.3, bf16[80,240]{1,0:T(8,128)(2,1)S(1)} %copy-done.2, bf16[256,256]{1,0:T(8,128)(2,1)S(1)} %copy-done.1, ...), custom_call_target="tpu_custom_call" | custom-call | tf_op jit(solution)/shard_map/pallas_call | solution.py:544
  108.0 1.7 %copy.14 = f32[1,128,1458]{1,0,2:T(1,128)} copy(f32[1,128,1458]{2,1,0:T(8,128)S(1)} %bitcast.5) | data formatting | bytes 1492992
  109.8 0.6 copy.19
Async XLA Ops:
  0.6 1.4 %copy-start = (bf16[256,256]{1,0:T(8,128)(2,1)S(1)}, bf16[256,256]{1,0:T(8,128)(2,1)}, u32[]{:S(2)}) copy-start(bf16[256,256]{1,0:T(8,128)(2,1)} %constant.60.tir) | copy-start | bytes 393220
  0.6 1.4 %copy-start.1 = (bf16[256,256]{1,0:T(8,128)(2,1)S(1)}, bf16[256,256]{1,0:T(8,128)(2,1)}, u32[]{:S(2)}) copy-start(bf16[256,256]{1,0:T(8,128)(2,1)} %constant.55.tr) | copy-start | bytes 393220
  0.7 1.4 %copy-start.2 = (bf16[80,240]{1,0:T(8,128)(2,1)S(1)}, bf16[80,240]{1,0:T(8,128)(2,1)}, u32[]{:S(2)}) copy-start(bf16[80,240]{1,0:T(8,128)(2,1)} %constant.50.til) | copy-start | bytes 115204
  0.7 1.4 %copy-start.3 = (bf16[80,240]{1,0:T(8,128)(2,1)S(1)}, bf16[80,240]{1,0:T(8,128)(2,1)}, u32[]{:S(2)}) copy-start(bf16[80,240]{1,0:T(8,128)(2,1)} %constant.43.tl) | copy-start | bytes 115204
  0.7 1.4 %copy-start.4 = (f32[80,128]{1,0:T(8,128)S(1)}, f32[80,128]{1,0:T(8,128)}, u32[]{:S(2)}) copy-start(f32[80,128]{1,0:T(8,128)} %constant.14.clone.sq_rows) | copy-start | bytes 122884
  0.7 1.4 %copy-start.5 = (f32[72,128]{1,0:T(8,128)S(1)}, f32[72,128]{1,0:T(8,128)}, u32[]{:S(2)}) copy-start(f32[72,128]{1,0:T(8,128)} %constant.15.clone.sq_pair) | copy-start | bytes 110596
  2.0 0.7 copy-start.6

commit v5 on v4

--- a/solution.py
+++ b/solution.py
@@ -70,7 +70,17 @@
     return jnp.concatenate([v, jnp.zeros((PAD - N, 128), F32)], axis=0)
 
 
-def spectra(own, lent, work, tl, til, tr, sq_rows, sq_pair, UA, UB):
+def fill_kernel(weight, sq_rows, sq_pair):
+    def one(b, carry):
+        total = sq_rows[...] + sq_pair[pl.ds(b, 1), :]
+        positive = total > 0
+        weight[b] = jnp.where(positive, (-0.25 * math.pi) / jnp.where(positive, total, 1.0), 0.0)
+        return carry
+
+    lax.fori_loop(0, N, one, 0)
+
+
+def spectra(own, lent, work, tl, til, tr, weight, UA, UB):
     lane = lax.broadcasted_iota(jnp.int32, (1, 128), 1) < N
 
     def stage_a(step, carry):
@@ -91,10 +101,7 @@
             planes = [pad_rows(work[pl.ds(b + i, N, stride=N), :]) for i in range(2)]
             planes = left_dot(tl[...], planes)
             for i in range(2):
-                total = sq_rows[...] + sq_pair[pl.ds(b + i, 1), :]
-                positive = total > 0
-                kern = jnp.where(positive, (-0.25 * math.pi) / jnp.where(positive, total, 1.0), 0.0)
-                planes[i] = planes[i] * kern
+                planes[i] = planes[i] * weight[b + i]
             planes = left_dot(til[...], planes)
             for i in range(2):
                 work[pl.ds(b + i, N, stride=N), :] = planes[i][:N]
@@ -197,6 +204,8 @@
 
 
 MET = 31 + 28
+FAR_Q = (8, 9, 7, 10, 6, 11, 5, 12, 4, 13, 3, 14, 2, 15, 1)
+FAR_P = (6, 2, 4, 5, 3, 7, 1)
 
 
 def lane_parts():
@@ -229,10 +238,12 @@
     keep_a2 = pltpu.make_async_copy(via_a.at[:, seat(me.q), :], cols.at[:, me.q, low], local.at[2])
     keep_b2 = pltpu.make_async_copy(via_b.at[:, me.p, :], cols.at[me.p, :, high], local.at[3])
 
-    for k in range(1, 8):
-        a1(k, lax.rem(me.p + k, 8), me.p).start()
-    for k in range(1, 16):
+    for n in range(15):
+        k = FAR_Q[n]
         b1(k, lax.rem(me.q + k, 16), slot).start()
+        if n % 2 == 0 and n < 14:
+            k = FAR_P[n // 2]
+            a1(k, lax.rem(me.p + k, 8), me.p).start()
 
     @pl.when(stays)
     def _():
@@ -256,7 +267,7 @@
         def _():
             a1(0, me.p, me.p).wait_recv()
 
-        for k in range(1, 16):
+        for k in FAR_Q:
             a2(k, lax.rem(me.q + k, 16), me.q).start()
         keep_a2.start()
 
@@ -272,7 +283,7 @@
         def _():
             b1(0, me.q, me.q).wait_recv()
 
-        for k in range(1, 8):
+        for k in FAR_P:
             b2(k, lax.rem(me.p + k, 8), me.p).start()
         keep_b2.start()
 
@@ -322,7 +333,7 @@
         )
 
     keep = pltpu.make_async_copy(picked.at[pl.ds(me.core, 1), :], cell(me.q), local)
-    for k in range(1, 16):
+    for k in FAR_Q:
         over_q(k, lax.rem(me.q + k, 16), me.q).start()
     keep.start()
     for k in range(1, 16):
@@ -389,66 +400,81 @@
     return drain
 
 
-def add_up(me, product, matrix, first, second, m_send, m_recv):
+def add_up(me, product, matrix, first, second, m_send, m_recv, meanwhile):
     p, q, grid = me.p, me.q, me.grid
+    where = 2 * p + grid
+    far = (12, 4, 13, 5, 8, 9, 10, 6, 11, 7, 14, 2, 15, 3, 1)
 
     def block(c):
         return pl.ds(pl.multiple_of(8 * c, 8), 8)
 
+    def ahead(k):
+        return lax.rem(p + k // 2, 8), lax.rem(grid + k, 2)
+
+    def behind(k):
+        return lax.rem(p + 8 - k // 2, 8), lax.rem(grid + k, 2)
+
     def scatter(k, to, slot):
-        return send(product.at[block(to), :], first.at[slot], m_send.at[k], m_recv.at[k], device(p, to, grid))
-
-    for k in range(1, 16):
-        scatter(k, lax.rem(q + k, 16), q).start()
-    first[q] = product[block(q), :]
-    for k in range(1, 16):
-        scatter(k, q, lax.rem(q + 16 - k, 16)).wait_recv()
+        return send(
+            product.at[block(2 * to[0] + to[1]), :], first.at[slot], m_send.at[k], m_recv.at[k], device(to[0], q, to[1])
+        )
+
+    for k in far:
+        scatter(k, ahead(k), where).start()
+    first[where] = product[block(where), :]
+    meanwhile()
+    for k in range(1, 16):
+        b = behind(k)
+        scatter(k, (p, grid), 2 * b[0] + b[1]).wait_recv()
     total = first[0]
     for k in range(1, 16):
         total = total + first[k]
-    where = 2 * p + grid
-    second[where] = total
-
-    def share(k, slot, p_to, g_to):
-        return send(second.at[slot], second.at[slot], m_send.at[15 + k], m_recv.at[15 + k], device(p_to, q, g_to))
-
-    for k in range(1, 16):
-        share(k, where, lax.rem(p + k // 2, 8), lax.rem(grid + k, 2)).start()
-    for k in range(1, 16):
-        p_, g_ = lax.rem(p + 8 - k // 2, 8), lax.rem(grid + k, 2)
-        share(k, 2 * p_ + g_, p_, g_).wait_recv()
+    second[q] = total
+
+    def share(k, slot, to):
+        return send(second.at[slot], second.at[slot], m_send.at[15 + k], m_recv.at[15 + k], device(p, to, grid))
+
+    for k in FAR_Q:
+        share(k, q, lax.rem(q + k, 16)).start()
+    for k in range(1, 16):
+        scatter(k, ahead(k), where).wait_send()
+    for k in range(1, 16):
+        share(k, lax.rem(q + 16 - k, 16), q).wait_recv()
     total = second[0]
     for k in range(1, 16):
         total = total + second[k]
-    matrix[block(q), :] = total
-
-    def spread(k, to, slot):
+    matrix[block(where), :] = total
+
+    def spread(k, slot, to):
         return send(
             matrix.at[block(slot), :], matrix.at[block(slot), :], m_send.at[30 + k], m_recv.at[30 + k],
-            device(p, to, grid),
+            device(to[0], q, to[1]),
         )
 
-    for k in range(1, 16):
-        spread(k, lax.rem(q + k, 16), q).start()
-    for k in range(1, 16):
-        spread(k, q, lax.rem(q + 16 - k, 16)).wait_recv()
-
-    for k in range(1, 16):
-        scatter(k, lax.rem(q + k, 16), q).wait_send()
-        share(k, where, lax.rem(p + k // 2, 8), lax.rem(grid + k, 2)).wait_send()
-        spread(k, lax.rem(q + k, 16), q).wait_send()
+    for k in far:
+        spread(k, where, ahead(k)).start()
+    for k in range(1, 16):
+        share(k, q, lax.rem(q + k, 16)).wait_send()
+    for k in range(1, 16):
+        b = behind(k)
+        spread(k, 2 * b[0] + b[1], (p, grid)).wait_recv()
+    for k in range(1, 16):
+        spread(k, where, ahead(k)).wait_send()
 
 
 def fock_kernel(
-    owners, orb, tl, til, tr, tir, sq_rows, sq_pair, field, matrix,
-    cols, whole, lent, blocks, picked, own_rows, lent_rows, work,
-    given, kept, arrived, product, first, second,
+    owners, orb_hbm, tl, til, tr, tir, sq_rows, sq_pair, field_out, matrix,
+    orb, weight, cols, whole, lent, blocks, picked, own_rows, lent_rows, work,
+    given, kept, arrived, field, turned, product, first, second,
     own_sem, w_send, w_recv, g_send, g_recv, t_send, t_recv, m_send, m_recv, *rest,
 ):
     near, far = rest[: len(rest) // 2], rest[len(rest) // 2 :]
     me = Place()
     partner = {"grid": 1 - me.grid}
+    load = pltpu.make_async_copy(orb_hbm.at[:, 0, :], orb, own_sem.at[0])
+    load.start()
     barrier = meet(me)
+    load.wait()
     from_plane(orb, work, 0)
     to_blocks(work, blocks, 0)
     pl.semaphore_wait(barrier, MET)
@@ -471,6 +497,7 @@
     def _():
         to_partner.start()
 
+    fill_kernel(weight, sq_rows, sq_pair)
     middle_a()
     middle_b()
     finish()
@@ -500,7 +527,7 @@
 
     for s in range(2):
         from_blocks(lent.at[s], lent_rows, s)
-    spectra(own_rows, lent_rows, work, tl, til, tr, sq_rows, sq_pair, 9, 9)
+    spectra(own_rows, lent_rows, work, tl, til, tr, weight, 9, 9)
     potentials(own_rows, lent_rows, work, til, tir, 1 - me.core, 9)
     to_blocks(own_rows, given, 1 - me.core)
     give = send(given, arrived, t_send, t_recv, me.twin)
@@ -513,6 +540,19 @@
     middle_a, middle_b, finish, drain_far = exchange(
         me, kept, far[0], far[1], field, 2 * me.z + me.grid, me.core, far[2:]
     )
+
+    @pl.when(same)
+    def _():
+        to_twin.wait_send()
+        forward.wait_send()
+
+    @pl.when(differ)
+    def _():
+        to_partner.wait_send()
+
+    give.wait_send()
+    drain_gather()
+    drain_near()
     middle_a()
     middle_b()
     finish()
@@ -520,21 +560,19 @@
     fh, fl = halves(field[...].reshape(BANDS, CELLS))
     dot = lambda a, b: lax.dot_general(a, b, (((1,), (1,)), ((), ())), preferred_element_type=F32)
     product[...] = ((dot(oh, fl) + dot(ol, fh)) + dot(oh, fh)) * (1.0 / 373248.0)
-    add_up(me, product, matrix, first, second, m_send, m_recv)
-
-    @pl.when(same)
-    def _():
-        to_twin.wait_send()
-        forward.wait_send()
-
-    @pl.when(differ)
-    def _():
-        to_partner.wait_send()
-
-    give.wait_send()
-    drain_gather()
-    drain_near()
-    drain_far()
+
+    store = pltpu.make_async_copy(turned, field_out.at[:, 0, :], own_sem.at[1])
+
+    def turn():
+        drain_far()
+        for n in range(12):
+            width = min(128, CELLS - 128 * n)
+            tile = field[:, :, pl.ds(128 * n, width)].reshape(BANDS, width)
+            turned[pl.ds(128 * n, width), :] = tile.T
+        store.start()
+
+    add_up(me, product, matrix, first, second, m_send, m_recv, turn)
+    store.wait()
 
 
 def fock_call(owners, orb):
@@ -544,24 +582,24 @@
     return pl.pallas_call(
         fock_kernel,
         out_shape=(
-            jax.ShapeDtypeStruct((8, 16, CELLS), F32),
+            jax.ShapeDtypeStruct((CELLS, 1, BANDS), F32),
             jax.ShapeDtypeStruct((BANDS, BANDS), F32),
         ),
-        in_specs=[pl.BlockSpec(memory_space=pltpu.SMEM)] + [vm] * 7,
-        out_specs=(vm, vm),
+        in_specs=[pl.BlockSpec(memory_space=pltpu.SMEM), pl.BlockSpec(memory_space=pl.ANY)] + [vm] * 6,
+        out_specs=(pl.BlockSpec(memory_space=pl.ANY), vm),
         scratch_shapes=[
-            v(8, 16, CELLS), v(2, 36, 5184), v(2, 2, 2, 32, CELLS), v(16, 8, CELLS), v(2, CELLS),
+            v(36, 5184), v(N, PAD, 128), v(8, 16, CELLS), v(2, 36, 5184), v(2, 2, 2, 32, CELLS), v(16, 8, CELLS), v(2, CELLS),
             v(5184, 128), v(5184, 128), v(5184, 128),
-            v(16, 8, CELLS), v(16, 8, CELLS), v(16, 8, CELLS), v(BANDS, BANDS), v(16, 8, BANDS), v(16, 8, BANDS),
+            v(16, 8, CELLS), v(16, 8, CELLS), v(16, 8, CELLS), v(8, 16, CELLS), v(CELLS, BANDS), v(BANDS, BANDS), v(16, 8, BANDS), v(16, 8, BANDS),
             dma((2,)), dma((2,)), dma((2,)), dma((56,)), dma((56,)), dma, dma, dma((46,)), dma((46,)),
         ] + exchange_scratch() + exchange_scratch(),
-        compiler_params=pltpu.CompilerParams(collective_id=0, has_side_effects=True, vmem_limit_bytes=48 << 20),
+        compiler_params=pltpu.CompilerParams(collective_id=0, has_side_effects=True, vmem_limit_bytes=60 << 20),
     )(owners, orb, *tables())
 
 
 def shards(orbitals, owners):
-    field, matrix = fock_call(owners, orbitals[0])
-    return (field.reshape(1, BANDS, CELLS), matrix)
+    field, matrix = fock_call(owners, orbitals.transpose(1, 0, 2))
+    return (field.transpose(1, 2, 0), matrix)
 
 
 def solution(mesh):

time: 110 us -> 106 us (0.964)
  Pallas kernels: 105 us -> 103 us
  local copies, waits for them, and re-layouts: 4.26 us -> 2.55 us
    pallas_call x1, Pallas kernels: 105 us -> 103 us  [fock_call(): pl.pallas_call(fock_kernel, out_shape=(jax.ShapeDtypeStruct((CELLS, 1, BA...]
    unnamed x17 -> x4, local copies, waits for them, and re-layouts: 4.26 us -> 2.55 us
where the time goes in v5:
time: 106 us
  Pallas kernels  103 us (97%)
  local copies, waits for them, and re-layouts  2.55 us (2%)
    pallas_call x1, Pallas kernels, fock_call(): pl.pallas_call(fock_kernel, out_shape=(jax.ShapeDtypeStruct((CELLS, 1, BA...  103 us
    unnamed x4, local copies, waits for them, and re-layouts  2.55 us

profile of v5, /device:TPU:1, one launch (start us, length us, event | category | flops | bytes accessed | tf_op | source)
XLA Modules:
  0.0 105.7 jit_solution(659318617459504078)
XLA Ops:
  0.6 102.5 %shard_map.131 = (f32[1458,1,128]{2,1,0:T(1,128)}, f32[128,128]{1,0:T(8,128)}) custom-call(s32[128]{0:T(128)} %owners.1, f32[36,1,5184]{2,1,0:T(1,128)} %bitcast.2, bf16[80,240]{1,0:T(8,128)(2,1)} %constant.43.tl, bf16[80,240]{1,0:T(8,128)(2,1)} %constant.50.til, bf16[256,256]{1,0:T(8,128)(2,1)} %constant.55.tr, bf16[256,256]{1,0:T(8,128)(2,1)} %constant.60.tir, ...), custom_call_target="tpu_custom_call" | custom-call | tf_op jit(solution)/shard_map/pallas_call | solution.py:582
  103.2 0.0 copy-start
  103.2 1.9 %copy.16 = f32[1,128,1458]{1,0,2:T(1,128)} copy(f32[1,128,1458]{1,0,2:T(1,128)} %bitcast.3) | data formatting | bytes 1492992
  105.1 0.0 copy-done
  105.1 0.6 copy.17
Async XLA Ops:
  103.2 1.9 %copy-start = (f32[128,128]{1,0:T(8,128)S(1)}, f32[128,128]{1,0:T(8,128)}, u32[]{:S(2)}) copy-start(f32[128,128]{1,0:T(8,128)} %get-tuple-element.9) | copy-start | bytes 196612

commit v6 on v5

--- a/solution.py
+++ b/solution.py
@@ -11,6 +11,7 @@
 
 N = 72
 PAD = 80
+GROUP = 9
 BF = jnp.bfloat16
 F32 = jnp.float32
 
@@ -84,13 +85,16 @@
     lane = lax.broadcasted_iota(jnp.int32, (1, 128), 1) < N
 
     def stage_a(step, carry):
-        for u in range(UA):
-            base = pl.multiple_of((step * UA + u) * 2 * N, 8)
-            rows = pl.ds(base, 2 * N)
+        span = 2 * N * GROUP
+        for u in range(UA // GROUP):
+            base = pl.multiple_of((step * (UA // GROUP) + u) * span, 8)
+            rows = pl.ds(base, span)
             d = jnp.where(lane, own[rows, :] * lent[rows, :], 0.0)
             z = right_dot(d, tr[...])
-            a, b = left_dot(tl[...], [pad_rows(z[:N]), pad_rows(z[N:])])
-            work[rows, :] = jnp.concatenate([a[:N], b[:N]], axis=0)
+            for n in range(GROUP):
+                at = 2 * N * n
+                planes = left_dot(tl[...], [pad_rows(z[at : at + N]), pad_rows(z[at + N : at + 2 * N])])
+                work[pl.ds(base + at, 2 * N), :] = jnp.concatenate([v[:N] for v in planes], axis=0)
         return carry
 
     lax.fori_loop(0, 36 // UA, stage_a, 0)
@@ -112,13 +116,15 @@
 
 def potentials(own, lent, work, til, tir, slab, UC):
     def stage_c(step, carry):
-        for u in range(UC):
-            base = pl.multiple_of(slab * 2592 + (step * UC + u) * 2 * N, 8)
-            rows = pl.ds(base, 2 * N)
-            v = work[rows, :]
-            a, b = left_dot(til[...], [pad_rows(v[:N]), pad_rows(v[N:])])
-            z = right_dot(jnp.concatenate([a[:N], b[:N]], axis=0), tir[...])
-            own[rows, :] = z * lent[rows, :]
+        span = 2 * N * GROUP
+        for u in range(UC // GROUP):
+            base = pl.multiple_of(slab * 2592 + (step * (UC // GROUP) + u) * span, 8)
+            planes = []
+            for n in range(GROUP):
+                v = work[pl.ds(base + 2 * N * n, 2 * N), :]
+                planes += left_dot(til[...], [pad_rows(v[:N]), pad_rows(v[N:])])
+            rows = pl.ds(base, span)
+            own[rows, :] = right_dot(jnp.concatenate([v[:N] for v in planes], axis=0), tir[...]) * lent[rows, :]
         return carry
 
     lax.fori_loop(0, 18 // UC, stage_c, 0)
@@ -287,12 +293,14 @@
             b2(k, lax.rem(me.p + k, 8), me.p).start()
         keep_b2.start()
 
-    def finish():
+    def finish_a():
         for k in range(1, 16):
             a2(k, me.q, lax.rem(me.q + 16 - k, 16)).wait_recv()
+        keep_a2.wait()
+
+    def finish_b():
         for k in range(1, 8):
             b2(k, me.p, lax.rem(me.p + 8 - k, 8)).wait_recv()
-        keep_a2.wait()
         keep_b2.wait()
 
     def drain():
@@ -308,7 +316,7 @@
             a1(0, me.p, me.p).wait_send()
             b1(0, me.q, slot).wait_send()
 
-    return middle_a, middle_b, finish, drain
+    return middle_a, middle_b, finish_a, finish_b, drain
 
 
 def exchange_scratch():
@@ -481,7 +489,7 @@
 
     same = me.core == me.grid
     differ = jnp.logical_not(same)
-    middle_a, middle_b, finish, drain_near = exchange(me, blocks, near[0], near[1], cols, me.q, me.grid, near[2:])
+    middle_a, middle_b, finish_a, finish_b, drain_near = exchange(me, blocks, near[0], near[1], cols, me.q, me.grid, near[2:])
     keep = pltpu.make_async_copy(orb, whole.at[me.grid], own_sem.at[0])
     to_twin = send(orb, whole.at[me.grid], w_send.at[0], w_recv.at[0], me.twin)
     to_partner = send(orb, whole.at[me.grid], w_send.at[0], w_recv.at[1], partner)
@@ -500,7 +508,8 @@
     fill_kernel(weight, sq_rows, sq_pair)
     middle_a()
     middle_b()
-    finish()
+    finish_a()
+    finish_b()
     for r in range(2):
         owner = owners[r]
         picked[r : r + 1, :] = cols[pl.ds(lax.div(owner, 16), 1), pl.ds(lax.rem(owner, 16), 1), :].reshape(1, CELLS)
@@ -527,17 +536,17 @@
 
     for s in range(2):
         from_blocks(lent.at[s], lent_rows, s)
-    spectra(own_rows, lent_rows, work, tl, til, tr, weight, 9, 9)
-    potentials(own_rows, lent_rows, work, til, tir, 1 - me.core, 9)
+    spectra(own_rows, lent_rows, work, tl, til, tr, weight, 36, 36)
+    potentials(own_rows, lent_rows, work, til, tir, 1 - me.core, 18)
     to_blocks(own_rows, given, 1 - me.core)
     give = send(given, arrived, t_send, t_recv, me.twin)
     give.start()
-    potentials(own_rows, lent_rows, work, til, tir, me.core, 9)
+    potentials(own_rows, lent_rows, work, til, tir, me.core, 18)
     to_blocks(own_rows, kept, me.core)
     give.wait_recv()
     kept[...] = kept[...] + arrived[...]
 
-    middle_a, middle_b, finish, drain_far = exchange(
+    middle_a, middle_b, finish_a, finish_b, drain_far = exchange(
         me, kept, far[0], far[1], field, 2 * me.z + me.grid, me.core, far[2:]
     )
 
@@ -555,12 +564,18 @@
     drain_near()
     middle_a()
     middle_b()
-    finish()
-    oh, ol = halves(cols[...].reshape(BANDS, CELLS))
-    fh, fl = halves(field[...].reshape(BANDS, CELLS))
     dot = lambda a, b: lax.dot_general(a, b, (((1,), (1,)), ((), ())), preferred_element_type=F32)
-    product[...] = ((dot(oh, fl) + dot(ol, fh)) + dot(oh, fh)) * (1.0 / 373248.0)
-
+
+    def overlap(lanes, width):
+        oh, ol = halves(cols[:, :, lanes].reshape(BANDS, width))
+        fh, fl = halves(field[:, :, lanes].reshape(BANDS, width))
+        return (dot(oh, fl) + dot(ol, fh)) + dot(oh, fh)
+
+    low, high = lane_parts()
+    finish_b()
+    product[...] = overlap(high, CELLS - CUT)
+    finish_a()
+    product[...] = (product[...] + overlap(low, CUT)) * (1.0 / 373248.0)
     store = pltpu.make_async_copy(turned, field_out.at[:, 0, :], own_sem.at[1])
 
     def turn():

time: 106 us -> 100 us (0.943)
  Pallas kernels: 103 us -> 97 us
    pallas_call x1, Pallas kernels: 103 us -> 97 us  [fock_call(): pl.pallas_call(fock_kernel, out_shape=(jax.ShapeDtypeStruct((CELLS, 1, BA...]
where the time goes in v6:
time: 100 us
  Pallas kernels  97 us (97%)
  local copies, waits for them, and re-layouts  2.55 us (3%)
    pallas_call x1, Pallas kernels, fock_call(): pl.pallas_call(fock_kernel, out_shape=(jax.ShapeDtypeStruct((CELLS, 1, BA...  97 us
    unnamed x4, local copies, waits for them, and re-layouts  2.55 us

profile of v6, /device:TPU:1, one launch (start us, length us, event | category | flops | bytes accessed | tf_op | source)
XLA Modules:
  0.0 100.2 jit_solution(17744341472910211659)
XLA Ops:
  0.6 97.0 %shard_map.131 = (f32[1458,1,128]{2,1,0:T(1,128)}, f32[128,128]{1,0:T(8,128)}) custom-call(s32[128]{0:T(128)} %owners.1, f32[36,1,5184]{2,1,0:T(1,128)} %bitcast.2, bf16[80,240]{1,0:T(8,128)(2,1)} %constant.43.tl, bf16[80,240]{1,0:T(8,128)(2,1)} %constant.50.til, bf16[256,256]{1,0:T(8,128)(2,1)} %constant.55.tr, bf16[256,256]{1,0:T(8,128)(2,1)} %constant.60.tir, ...), custom_call_target="tpu_custom_call" | custom-call | tf_op jit(solution)/shard_map/pallas_call | solution.py:597
  97.7 0.0 copy-start
  97.7 1.9 %copy.16 = f32[1,128,1458]{1,0,2:T(1,128)} copy(f32[1,128,1458]{1,0,2:T(1,128)} %bitcast.3) | data formatting | bytes 1492992
  99.6 0.0 copy-done
  99.6 0.6 copy.17
Async XLA Ops:
  97.7 1.9 %copy-start = (f32[128,128]{1,0:T(8,128)S(1)}, f32[128,128]{1,0:T(8,128)}, u32[]{:S(2)}) copy-start(f32[128,128]{1,0:T(8,128)} %get-tuple-element.9) | copy-start | bytes 196612

commit v7 on v6

--- a/solution.py
+++ b/solution.py
@@ -378,26 +378,39 @@
         copy.start()
         started.append(copy)
 
-    for n in range(1, 4):
+    def second(m, xh, grid):
+        for n in (2, 1, 3) if m == 3 else (1, 3):
+            go(along_y(24 + 4 * m, 0, xh, grid, n))
+            go(along_x(40 + 4 * m, 1, lax.rem(me.y + 4 - m, 4), n))
+
+    for n in (2, 1, 3):
         go(along_x(16, 0, me.y, n))
         go(along_y(20, 1, me.xh, me.grid, n))
-    for n in range(1, 4):
-        go(along_y(24, 0, me.xh, me.grid, n))
-        go(along_x(40, 1, me.y, n))
+    second(0, me.xh, me.grid)
     for m in range(1, 4):
         from_x(16, 0, me.y, m).wait_recv()
+        from_y(20, 1, me.xh, me.grid, m).wait_recv()
+        second(m, *x_peer(m))
+    for m in range(3):
+        near, away = (1, 3) if m % 2 == 0 else (3, 1)
         xh, grid = x_peer(m)
-        for n in range(1, 4):
-            go(along_y(24 + 4 * m, 0, xh, grid, n))
-        from_y(20, 1, me.xh, me.grid, m).wait_recv()
-        for n in range(1, 4):
-            go(along_x(40 + 4 * m, 1, lax.rem(me.y + 4 - m, 4), n))
+        y_m = lax.rem(me.y + 4 - m, 4)
+        from_y(24 + 4 * m, 0, xh, grid, near).wait_recv()
+        part = piece(0, grid, xh, lax.rem(me.y + 4 - near, 4))
+        go(send(part, part, send_sem.at[26 + 4 * m], recv_sem.at[26 + 4 * m],
+                device(4 * me.xh + lax.rem(me.y + near, 4), me.q, me.grid)))
+        from_x(40 + 4 * m, 1, y_m, near).wait_recv()
+        xh_near, grid_near = x_peer(near)
+        xh_away, grid_away = x_peer(away)
+        part = piece(1, grid_near, xh_near, y_m)
+        go(send(part, part, send_sem.at[42 + 4 * m], recv_sem.at[42 + 4 * m], device(4 * xh_away + me.y, me.q, grid_away)))
     meanwhile()
     for m in range(4):
         xh, grid = x_peer(m)
-        for n in range(1, 4):
+        y_m = lax.rem(me.y + 4 - m, 4)
+        for n in (1, 3, 2) if m == 3 else ((3, 2) if m % 2 == 0 else (1, 2)):
             from_y(24 + 4 * m, 0, xh, grid, n).wait_recv()
-            from_x(40 + 4 * m, 1, lax.rem(me.y + 4 - m, 4), n).wait_recv()
+            from_x(40 + 4 * m, 1, y_m, n).wait_recv()
 
     def drain():
         for k in range(1, 16):
@@ -612,8 +625,31 @@
     )(owners, orb, *tables())
 
 
+def result_kernel(field, matrix, field_out, matrix_out, sems):
+    copies = [pltpu.make_async_copy(matrix, matrix_out, sems.at[6])]
+    for n in range(6):
+        rows = pl.ds(243 * n, 243)
+        copies.append(pltpu.make_async_copy(field.at[rows], field_out.at[rows], sems.at[n]))
+    for c in copies:
+        c.start()
+    for c in copies:
+        c.wait()
+
+
+def result_call(field, matrix):
+    hbm = pl.BlockSpec(memory_space=pl.ANY)
+    return pl.pallas_call(
+        result_kernel,
+        out_shape=(jax.ShapeDtypeStruct(field.shape, F32), jax.ShapeDtypeStruct(matrix.shape, F32)),
+        in_specs=[hbm, hbm],
+        out_specs=(hbm, hbm),
+        scratch_shapes=[pltpu.SemaphoreType.DMA((7,))],
+    )(field, matrix)
+
+
 def shards(orbitals, owners):
     field, matrix = fock_call(owners, orbitals.transpose(1, 0, 2))
+    field, matrix = result_call(field, matrix)
     return (field.transpose(1, 2, 0), matrix)
 
 

time: 100 us -> 124 us (1.24)
  Pallas kernels: 97 us -> 124 us
  local copies, waits for them, and re-layouts: 2.55 us -> 0 us
    pallas_call x0 -> x1, Pallas kernels: none -> 25.8 us  [result_call(): pl.pallas_call(result_kernel, out_shape=(jax.ShapeDtypeStruct(field.shape...]
    unnamed x4 -> x0, local copies, waits for them, and re-layouts: 2.55 us -> none
where the time goes in v7:
time: 124 us
  Pallas kernels  124 us (100%)
    pallas_call x1, Pallas kernels, fock_call(): pl.pallas_call(fock_kernel, out_shape=(jax.ShapeDtypeStruct((CELLS, 1, BA...  98 us
    pallas_call x1, Pallas kernels, result_call(): pl.pallas_call(result_kernel, out_shape=(jax.ShapeDtypeStruct(field.shape...  25.8 us

profile of v7, /device:TPU:1, one launch (start us, length us, event | category | flops | bytes accessed | tf_op | source)
XLA Modules:
  0.0 124.4 jit_solution(6308822270313107794)
XLA Ops:
  0.6 98.0 %shard_map.131 = (f32[1458,1,128]{2,1,0:T(1,128)}, f32[128,128]{1,0:T(8,128)}) custom-call(s32[128]{0:T(128)} %owners.1, f32[36,1,5184]{2,1,0:T(1,128)} %bitcast.2, bf16[80,240]{1,0:T(8,128)(2,1)} %constant.43.tl, bf16[80,240]{1,0:T(8,128)(2,1)} %constant.50.til, bf16[256,256]{1,0:T(8,128)(2,1)} %constant.55.tr, bf16[256,256]{1,0:T(8,128)(2,1)} %constant.60.tir, ...), custom_call_target="tpu_custom_call" | custom-call | tf_op jit(solution)/shard_map/pallas_call | solution.py:610
  98.6 25.8 %shard_map.132 = (f32[1458,1,128]{2,1,0:T(1,128)}, f32[128,128]{1,0:T(8,128)}) custom-call(f32[1458,1,128]{2,1,0:T(1,128)} %get-tuple-element.6.field, f32[128,128]{1,0:T(8,128)} %get-tuple-element.7.matrix), custom_call_target="tpu_custom_call" | custom-call | tf_op jit(solution)/shard_map/pallas_call | solution.py:641

commit v8 on v6

--- a/solution.py
+++ b/solution.py
@@ -114,11 +114,11 @@
     lax.fori_loop(0, 36 // UB, stage_b, 0)
 
 
-def potentials(own, lent, work, til, tir, slab, UC):
+def potentials(own, lent, work, til, tir, row, UC, pairs):
     def stage_c(step, carry):
         span = 2 * N * GROUP
         for u in range(UC // GROUP):
-            base = pl.multiple_of(slab * 2592 + (step * (UC // GROUP) + u) * span, 8)
+            base = pl.multiple_of(row + (step * (UC // GROUP) + u) * span, 8)
             planes = []
             for n in range(GROUP):
                 v = work[pl.ds(base + 2 * N * n, 2 * N), :]
@@ -127,7 +127,7 @@
             own[rows, :] = right_dot(jnp.concatenate([v[:N] for v in planes], axis=0), tir[...]) * lent[rows, :]
         return carry
 
-    lax.fori_loop(0, 18 // UC, stage_c, 0)
+    lax.fori_loop(0, pairs // UC, stage_c, 0)
 
 
 def from_plane(ref, dst, slab):
@@ -151,13 +151,13 @@
         dst[rows, :N] = v
 
 
-def to_blocks(src, ref, slab):
+def to_blocks(src, ref, row, count, place):
     for h in range(4):
         for j, first, at, fit in spans():
-            v = src[pl.ds(slab * 2592 + 81 * h + j, 8, stride=324), :]
-            ref[4 * first + h, :, at : at + fit] = v[:, :fit]
+            v = src[pl.ds(row + 81 * h + j, count, stride=324), :]
+            ref[4 * first + h, place : place + count, at : at + fit] = v[:, :fit]
             if fit < N:
-                ref[4 * first + 4 + h, :, : N - fit] = v[:, fit:N]
+                ref[4 * first + 4 + h, place : place + count, : N - fit] = v[:, fit:N]
 
 
 MESH = pl.DeviceIdType.MESH
@@ -218,7 +218,7 @@
     return pl.ds(0, CUT), pl.ds(CUT, CELLS - CUT)
 
 
-def exchange(me, blocks, via_a, via_b, cols, slot, grid_to, sems):
+def exchange(me, blocks, via_a, via_b, cols, slot, grid_to, sems, parts):
     s1, r1, s2, r2, s3, r3, s4, r4, local = sems
     low, high = lane_parts()
     stays = jnp.logical_and(slot == me.q, grid_to == me.grid)
@@ -230,8 +230,14 @@
     def a1(k, p_to, p_from):
         return send(blocks.at[:, p_to, low], via_a.at[p_from], s1.at[k], r1.at[k], device(p_to, slot, grid_to))
 
-    def b1(k, q_to, q_from):
-        return send(blocks.at[seat(q_to), :, high], via_b.at[q_from], s2.at[k], r2.at[q_from], device(me.p, q_to, grid_to))
+    def rows(part):
+        return pl.ds(8 // parts * part, 8 // parts)
+
+    def b1(part, k, q_to, q_from):
+        return send(
+            blocks.at[seat(q_to), rows(part), high], via_b.at[q_from, rows(part), :],
+            s2.at[16 * part + k], r2.at[16 * part + q_from], device(me.p, q_to, grid_to),
+        )
 
     def a2(k, q_to, q_from):
         return send(via_a.at[:, seat(q_to), :], cols.at[:, q_from, low], s3.at[k], r3.at[k], device(me.p, q_to, me.grid))
@@ -240,26 +246,47 @@
         return send(via_b.at[:, p_to, :], cols.at[p_from, :, high], s4.at[k], r4.at[k], device(p_to, me.q, me.grid))
 
     keep_a1 = pltpu.make_async_copy(blocks.at[:, me.p, low], via_a.at[me.p], local.at[0])
-    keep_b1 = pltpu.make_async_copy(blocks.at[seat(me.q), :, high], via_b.at[me.q], local.at[1])
+    def keep_b1(part):
+        return pltpu.make_async_copy(
+            blocks.at[seat(me.q), rows(part), high], via_b.at[me.q, rows(part), :], local.at[4 * part + 1]
+        )
+
     keep_a2 = pltpu.make_async_copy(via_a.at[:, seat(me.q), :], cols.at[:, me.q, low], local.at[2])
     keep_b2 = pltpu.make_async_copy(via_b.at[:, me.p, :], cols.at[me.p, :, high], local.at[3])
 
-    for n in range(15):
-        k = FAR_Q[n]
-        b1(k, lax.rem(me.q + k, 16), slot).start()
-        if n % 2 == 0 and n < 14:
-            k = FAR_P[n // 2]
-            a1(k, lax.rem(me.p + k, 8), me.p).start()
-
-    @pl.when(stays)
-    def _():
-        keep_a1.start()
-        keep_b1.start()
-
-    @pl.when(moves)
-    def _():
-        a1(0, me.p, me.p).start()
-        b1(0, me.q, slot).start()
+    def begin(part):
+        for n in range(15):
+            k = FAR_Q[n]
+            b1(part, k, lax.rem(me.q + k, 16), slot).start()
+            if parts == 1 and n % 2 == 0 and n < 14:
+                k = FAR_P[n // 2]
+                a1(k, lax.rem(me.p + k, 8), me.p).start()
+            if parts == 2 and n % 4 == 1 and n < 10:
+                p_to = 4 * part + lax.rem(me.y + (2, 1, 3)[n // 4], 4)
+                a1(lax.rem(p_to + 8 - me.p, 8), p_to, me.p).start()
+
+        @pl.when(stays)
+        def _():
+            keep_b1(part).start()
+
+        @pl.when(moves)
+        def _():
+            b1(part, 0, me.q, slot).start()
+
+        here = (part == me.xh) if parts == 2 else True
+
+        @pl.when(jnp.logical_and(stays, here))
+        def _():
+            keep_a1.start()
+
+        @pl.when(jnp.logical_and(moves, here))
+        def _():
+            a1(0, me.p, me.p).start()
+
+        if parts == 2:
+            @pl.when(jnp.logical_not(here))
+            def _():
+                a1(4, lax.rem(me.p + 4, 8), me.p).start()
 
     def middle_a():
         for k in range(1, 8):
@@ -278,16 +305,19 @@
         keep_a2.start()
 
     def middle_b():
-        for k in range(1, 16):
-            b1(k, me.q, lax.rem(me.q + k, 16)).wait_recv()
+        for part in range(parts):
+            for k in range(1, 16):
+                b1(part, k, me.q, lax.rem(me.q + k, 16)).wait_recv()
 
         @pl.when(stays)
         def _():
-            keep_b1.wait()
+            for part in range(parts):
+                keep_b1(part).wait()
 
         @pl.when(moves)
         def _():
-            b1(0, me.q, me.q).wait_recv()
+            for part in range(parts):
+                b1(part, 0, me.q, me.q).wait_recv()
 
         for k in FAR_P:
             b2(k, lax.rem(me.p + k, 8), me.p).start()
@@ -308,22 +338,24 @@
             a1(k, lax.rem(me.p + k, 8), me.p).wait_send()
             b2(k, lax.rem(me.p + k, 8), me.p).wait_send()
         for k in range(1, 16):
-            b1(k, lax.rem(me.q + k, 16), slot).wait_send()
+            for part in range(parts):
+                b1(part, k, lax.rem(me.q + k, 16), slot).wait_send()
             a2(k, lax.rem(me.q + k, 16), me.q).wait_send()
 
         @pl.when(moves)
         def _():
             a1(0, me.p, me.p).wait_send()
-            b1(0, me.q, slot).wait_send()
-
-    return middle_a, middle_b, finish_a, finish_b, drain
+            for part in range(parts):
+                b1(part, 0, me.q, slot).wait_send()
+
+    return begin, middle_a, middle_b, finish_a, finish_b, drain
 
 
 def exchange_scratch():
     dma = pltpu.SemaphoreType.DMA
     return [
         pltpu.VMEM((8, 16, CUT), F32), pltpu.VMEM((16, 8, CELLS - CUT), F32),
-        dma((8,)), dma((8,)), dma((16,)), dma((16,)), dma((16,)), dma((16,)), dma((8,)), dma((8,)), dma((4,)),
+        dma((8,)), dma((8,)), dma((32,)), dma((32,)), dma((16,)), dma((16,)), dma((8,)), dma((8,)), dma((6,)),
     ]
 
 
@@ -484,12 +516,15 @@
     barrier = meet(me)
     load.wait()
     from_plane(orb, work, 0)
-    to_blocks(work, blocks, 0)
+    to_blocks(work, blocks, 0, 8, 0)
     pl.semaphore_wait(barrier, MET)
 
     same = me.core == me.grid
     differ = jnp.logical_not(same)
-    middle_a, middle_b, finish_a, finish_b, drain_near = exchange(me, blocks, near[0], near[1], cols, me.q, me.grid, near[2:])
+    begin, middle_a, middle_b, finish_a, finish_b, drain_near = exchange(
+        me, blocks, near[0], near[1], cols, me.q, me.grid, near[2:], 1
+    )
+    begin(0)
     keep = pltpu.make_async_copy(orb, whole.at[me.grid], own_sem.at[0])
     to_twin = send(orb, whole.at[me.grid], w_send.at[0], w_recv.at[0], me.twin)
     to_partner = send(orb, whole.at[me.grid], w_send.at[0], w_recv.at[1], partner)
@@ -537,18 +572,28 @@
     for s in range(2):
         from_blocks(lent.at[s], lent_rows, s)
     spectra(own_rows, lent_rows, work, tl, til, tr, weight, 36, 36)
-    potentials(own_rows, lent_rows, work, til, tir, 1 - me.core, 18)
-    to_blocks(own_rows, given, 1 - me.core)
-    give = send(given, arrived, t_send, t_recv, me.twin)
-    give.start()
-    potentials(own_rows, lent_rows, work, til, tir, me.core, 18)
-    to_blocks(own_rows, kept, me.core)
-    give.wait_recv()
-    kept[...] = kept[...] + arrived[...]
-
-    middle_a, middle_b, finish_a, finish_b, drain_far = exchange(
-        me, kept, far[0], far[1], field, 2 * me.z + me.grid, me.core, far[2:]
+    begin, middle_a, middle_b, finish_a, finish_b, drain_far = exchange(
+        me, kept, far[0], far[1], field, 2 * me.z + me.grid, me.core, far[2:], 2
     )
+
+    def give(part):
+        piece = pl.ds(4 * part, 4)
+        return send(given.at[:, piece, :], arrived.at[:, piece, :], t_send.at[part], t_recv.at[part], me.twin)
+
+    for part in range(2):
+        row = (1 - me.core) * 2592 + part * 1296
+        potentials(own_rows, lent_rows, work, til, tir, row, 9, 9)
+        to_blocks(own_rows, given, row, 4, 4 * part)
+        give(part).start()
+    for part in range(2):
+        row = me.core * 2592 + part * 1296
+        potentials(own_rows, lent_rows, work, til, tir, row, 9, 9)
+        to_blocks(own_rows, kept, row, 4, 4 * part)
+    for part in range(2):
+        give(part).wait_recv()
+        at = slice(4 * part, 4 * part + 4)
+        kept[:, at, :] = kept[:, at, :] + arrived[:, at, :]
+        begin(part)
 
     @pl.when(same)
     def _():
@@ -559,7 +604,8 @@
     def _():
         to_partner.wait_send()
 
-    give.wait_send()
+    for part in range(2):
+        give(part).wait_send()
     drain_gather()
     drain_near()
     middle_a()
@@ -606,7 +652,7 @@
             v(36, 5184), v(N, PAD, 128), v(8, 16, CELLS), v(2, 36, 5184), v(2, 2, 2, 32, CELLS), v(16, 8, CELLS), v(2, CELLS),
             v(5184, 128), v(5184, 128), v(5184, 128),
             v(16, 8, CELLS), v(16, 8, CELLS), v(16, 8, CELLS), v(8, 16, CELLS), v(CELLS, BANDS), v(BANDS, BANDS), v(16, 8, BANDS), v(16, 8, BANDS),
-            dma((2,)), dma((2,)), dma((2,)), dma((56,)), dma((56,)), dma, dma, dma((46,)), dma((46,)),
+            dma((2,)), dma((2,)), dma((2,)), dma((56,)), dma((56,)), dma((2,)), dma((2,)), dma((46,)), dma((46,)),
         ] + exchange_scratch() + exchange_scratch(),
         compiler_params=pltpu.CompilerParams(collective_id=0, has_side_effects=True, vmem_limit_bytes=60 << 20),
     )(owners, orb, *tables())

time: 100 us -> 101 us (1.010)
  Pallas kernels: 97 us -> 98.1 us
    pallas_call x1, Pallas kernels: 97 us -> 98.1 us  [fock_call(): pl.pallas_call(fock_kernel, out_shape=(jax.ShapeDtypeStruct((CELLS, 1, BA...]
where the time goes in v8:
time: 101 us
  Pallas kernels  98.1 us (97%)
  local copies, waits for them, and re-layouts  2.55 us (3%)
    pallas_call x1, Pallas kernels, fock_call(): pl.pallas_call(fock_kernel, out_shape=(jax.ShapeDtypeStruct((CELLS, 1, BA...  98.1 us
    unnamed x4, local copies, waits for them, and re-layouts  2.55 us

profile of v8, /device:TPU:1, one launch (start us, length us, event | category | flops | bytes accessed | tf_op | source)
XLA Modules:
  0.0 101.3 jit_solution(17233834155636204142)
XLA Ops:
  0.6 98.1 %shard_map.131 = (f32[1458,1,128]{2,1,0:T(1,128)}, f32[128,128]{1,0:T(8,128)}) custom-call(s32[128]{0:T(128)} %owners.1, f32[36,1,5184]{2,1,0:T(1,128)} %bitcast.2, bf16[80,240]{1,0:T(8,128)(2,1)} %constant.43.tl, bf16[80,240]{1,0:T(8,128)(2,1)} %constant.50.til, bf16[256,256]{1,0:T(8,128)(2,1)} %constant.55.tr, bf16[256,256]{1,0:T(8,128)(2,1)} %constant.60.tir, ...), custom_call_target="tpu_custom_call" | custom-call | tf_op jit(solution)/shard_map/pallas_call | solution.py:643
  98.7 0.0 copy-start
  98.7 1.9 %copy.16 = f32[1,128,1458]{1,0,2:T(1,128)} copy(f32[1,128,1458]{1,0,2:T(1,128)} %bitcast.3) | data formatting | bytes 1492992
  100.7 0.0 copy-done
  100.7 0.6 copy.17
Async XLA Ops:
  98.7 1.9 %copy-start = (f32[128,128]{1,0:T(8,128)S(1)}, f32[128,128]{1,0:T(8,128)}, u32[]{:S(2)}) copy-start(f32[128,128]{1,0:T(8,128)} %get-tuple-element.9) | copy-start | bytes 196612

commit v9 on v6

--- a/solution.py
+++ b/solution.py
@@ -378,19 +378,19 @@
         copy.start()
         started.append(copy)
 
-    for n in range(1, 4):
+    for n in (2, 1, 3):
         go(along_x(16, 0, me.y, n))
         go(along_y(20, 1, me.xh, me.grid, n))
-    for n in range(1, 4):
+    for n in (2, 1, 3):
         go(along_y(24, 0, me.xh, me.grid, n))
         go(along_x(40, 1, me.y, n))
     for m in range(1, 4):
         from_x(16, 0, me.y, m).wait_recv()
         xh, grid = x_peer(m)
-        for n in range(1, 4):
+        for n in (2, 1, 3):
             go(along_y(24 + 4 * m, 0, xh, grid, n))
         from_y(20, 1, me.xh, me.grid, m).wait_recv()
-        for n in range(1, 4):
+        for n in (2, 1, 3):
             go(along_x(40 + 4 * m, 1, lax.rem(me.y + 4 - m, 4), n))
     meanwhile()
     for m in range(4):

time: 100 us -> 99.9 us (level)
  no operation moved by 1% of the time
where the time goes in v9:
time: 99.9 us; the launch traced here: 99.7 us
  Pallas kernels  96.5 us (97%)
  local copies, waits for them, and re-layouts  2.55 us (3%)
    pallas_call x1, Pallas kernels, fock_call(): pl.pallas_call(fock_kernel, out_shape=(jax.ShapeDtypeStruct((CELLS, 1, BA...  96.5 us
    unnamed x4, local copies, waits for them, and re-layouts  2.55 us

profile of v9, /device:TPU:1, one launch (start us, length us, event | category | flops | bytes accessed | tf_op | source)
XLA Modules:
  0.0 99.7 jit_solution(13105252496549108459)
XLA Ops:
  0.6 96.5 %shard_map.131 = (f32[1458,1,128]{2,1,0:T(1,128)}, f32[128,128]{1,0:T(8,128)}) custom-call(s32[128]{0:T(128)} %owners.1, f32[36,1,5184]{2,1,0:T(1,128)} %bitcast.2, bf16[80,240]{1,0:T(8,128)(2,1)} %constant.43.tl, bf16[80,240]{1,0:T(8,128)(2,1)} %constant.50.til, bf16[256,256]{1,0:T(8,128)(2,1)} %constant.55.tr, bf16[256,256]{1,0:T(8,128)(2,1)} %constant.60.tir, ...), custom_call_target="tpu_custom_call" | custom-call | tf_op jit(solution)/shard_map/pallas_call | solution.py:597
  97.2 0.0 copy-start
  97.2 1.9 %copy.16 = f32[1,128,1458]{1,0,2:T(1,128)} copy(f32[1,128,1458]{1,0,2:T(1,128)} %bitcast.3) | data formatting | bytes 1492992
  99.1 0.0 copy-done
  99.1 0.6 copy.17
Async XLA Ops:
  97.2 1.9 %copy-start = (f32[128,128]{1,0:T(8,128)S(1)}, f32[128,128]{1,0:T(8,128)}, u32[]{:S(2)}) copy-start(f32[128,128]{1,0:T(8,128)} %get-tuple-element.9) | copy-start | bytes 196612

commit v10 on v9

--- a/solution.py
+++ b/solution.py
@@ -501,12 +501,13 @@
         keep.start()
         to_twin.start()
 
+    fill_kernel(weight, sq_rows, sq_pair)
+    middle_a()
+
     @pl.when(differ)
     def _():
         to_partner.start()
 
-    fill_kernel(weight, sq_rows, sq_pair)
-    middle_a()
     middle_b()
     finish_a()
     finish_b()

time: 99.9 us -> 104 us (1.041)
  Pallas kernels: 96.5 us -> 101 us
    pallas_call x1, Pallas kernels: 96.5 us -> 101 us  [fock_call(): pl.pallas_call(fock_kernel, out_shape=(jax.ShapeDtypeStruct((CELLS, 1, BA...]
where the time goes in v10:
time: 104 us
  Pallas kernels  101 us (97%)
  local copies, waits for them, and re-layouts  2.55 us (2%)
    pallas_call x1, Pallas kernels, fock_call(): pl.pallas_call(fock_kernel, out_shape=(jax.ShapeDtypeStruct((CELLS, 1, BA...  101 us
    unnamed x4, local copies, waits for them, and re-layouts  2.55 us

profile of v10, /device:TPU:1, one launch (start us, length us, event | category | flops | bytes accessed | tf_op | source)
XLA Modules:
  0.0 104.1 jit_solution(5209424803555255711)
XLA Ops:
  0.6 100.9 %shard_map.131 = (f32[1458,1,128]{2,1,0:T(1,128)}, f32[128,128]{1,0:T(8,128)}) custom-call(s32[128]{0:T(128)} %owners.1, f32[36,1,5184]{2,1,0:T(1,128)} %bitcast.2, bf16[80,240]{1,0:T(8,128)(2,1)} %constant.43.tl, bf16[80,240]{1,0:T(8,128)(2,1)} %constant.50.til, bf16[256,256]{1,0:T(8,128)(2,1)} %constant.55.tr, bf16[256,256]{1,0:T(8,128)(2,1)} %constant.60.tir, ...), custom_call_target="tpu_custom_call" | custom-call | tf_op jit(solution)/shard_map/pallas_call | solution.py:598
  101.6 0.0 copy-start
  101.6 1.9 %copy.16 = f32[1,128,1458]{1,0,2:T(1,128)} copy(f32[1,128,1458]{1,0,2:T(1,128)} %bitcast.3) | data formatting | bytes 1492992
  103.5 0.0 copy-done
  103.5 0.6 copy.17
Async XLA Ops:
  101.6 1.9 %copy-start = (f32[128,128]{1,0:T(8,128)S(1)}, f32[128,128]{1,0:T(8,128)}, u32[]{:S(2)}) copy-start(f32[128,128]{1,0:T(8,128)} %get-tuple-element.9) | copy-start | bytes 196612
